TPU v7x, 32 devices: a whole 2x2x4 slice. The times are simulated.
32 devices in a mesh: row: 4 (over y, x), col: 8 (over z, core).
Axes of the slice: x: 2, y: 2, z: 4, core: 2. Of those that a mesh axis runs over, the one named last changes fastest.
Arguments:
- initial_kelvin_state: float32 [8, 512, 1024], P(None, 'row', 'col'), may hold values from -6 to 6
- substance_region: int32 [8, 512, 1024], P(None, 'row', 'col'), may hold values from 0 to 2, as said below
- source_energy: float32 [8, 512, 1024], P(None, 'row', 'col'), may hold values from 0.2 to 5
- substance_transfer_magnitude: float32 [3], replicated, may hold values from 0.02 to 6, as said below
- substance_softening_rate: float32 [3], replicated, may hold values from 0.05 to 0.25
Outputs:
- new_temperature: float32 [8, 512, 1024], P(None, 'row', 'col')
Inputs may be any that keep to these rules, and one draw needn't show every extreme that they name: `substance_region`: 0 die, 1 thermal interface material, 2 spreader. `substance_transfer_magnitude`: positive conductivity scales of die, interface material and spreader, in that order.
All inputs are finite; a program needn't handle non-finite values.
Results may differ from a plain program's by a relative error of at most 0.0027.
Values sent between devices are 32-bit elements; how exact they have to be, the bound alone decides.
A program may use at most 192 MiB of HBM per device.

v0:
```python
import jax
import jax.numpy as jnp
from jax import lax
from jax.sharding import PartitionSpec as P

inplane_ratio = 1000.0
depth_ratio = 0.08


def padded_2(cells, sides, width):
    for axis, dim in sides:
        count = lax.axis_size(axis)
        ends = count - 1
        head = lax.slice_in_dim(cells, 0, width, axis=dim)
        tail = lax.slice_in_dim(cells, cells.shape[dim] - width, cells.shape[dim], axis=dim)
        cells = jnp.concatenate(
            [
                lax.ppermute(tail, axis, [(i, (i + 1) % count) for i in range(ends)]),
                cells,
                lax.ppermute(head, axis, [((i + 1) % count, i) for i in range(ends)]),
            ],
            axis=dim,
        )
    return cells


def transfer_coefficient_array(
    initial_kelvin_state, substance_region, substance_transfer_magnitude, substance_softening_rate
):
    nodal_transfer_coefficient = jnp.where(
        substance_region == 0,
        substance_transfer_magnitude[0],
        jnp.where(
            substance_region == 1, substance_transfer_magnitude[1], substance_transfer_magnitude[2]
        ),
    )
    nodal_thermal_softening = jnp.where(
        substance_region == 0,
        substance_softening_rate[0],
        jnp.where(substance_region == 1, substance_softening_rate[1], substance_softening_rate[2]),
    )
    return nodal_transfer_coefficient * jnp.exp(-nodal_thermal_softening * initial_kelvin_state)


def face_conductance(center, beside):
    return 2.0 * center * beside / (center + beside)


def forward_diffusion_parts(field_padded, cond_padded):
    field_center = field_padded[:, 1:-1, 1:-1]
    cond_center = cond_padded[:, 1:-1, 1:-1]

    def flux(field_beside, cond_beside):
        return face_conductance(cond_center, cond_beside) * (field_beside - field_center)

    implicit_pass_first_axis = inplane_ratio * (
        flux(field_padded[:, 1:-1, 2:], cond_padded[:, 1:-1, 2:])
        + flux(field_padded[:, 1:-1, :-2], cond_padded[:, 1:-1, :-2])
    )
    implicit_pass_second_axis = inplane_ratio * (
        flux(field_padded[:, 2:, 1:-1], cond_padded[:, 2:, 1:-1])
        + flux(field_padded[:, :-2, 1:-1], cond_padded[:, :-2, 1:-1])
    )
    field_layers = jnp.pad(field_center, ((1, 1), (0, 0), (0, 0)))
    cond_layers = jnp.pad(cond_center, ((1, 1), (0, 0), (0, 0)))
    implicit_pass_third_axis = depth_ratio * (
        flux(field_layers[2:], cond_layers[2:]) + flux(field_layers[:-2], cond_layers[:-2])
    )
    bottom = (lax.broadcasted_iota(jnp.int32, field_center.shape, 0) == 0).astype(
        field_center.dtype
    )
    implicit_pass_third_axis = (
        implicit_pass_third_axis - depth_ratio * bottom * cond_center * field_center
    )
    return (implicit_pass_first_axis, implicit_pass_second_axis, implicit_pass_third_axis)


def line_system(cond_lines, line_axis, ratio):
    length = cond_lines.shape[line_axis]
    plate_thicknesses = [(0, 0)] * cond_lines.ndim
    plate_thicknesses[line_axis] = (1, 1)
    cond_padded = jnp.pad(cond_lines, plate_thicknesses)
    before = lax.slice_in_dim(cond_padded, 0, length, axis=line_axis)
    after = lax.slice_in_dim(cond_padded, 2, length + 2, axis=line_axis)
    lower_band = -0.5 * ratio * face_conductance(cond_lines, before)
    upper_band = -0.5 * ratio * face_conductance(cond_lines, after)
    main_band = 1.0 - lower_band - upper_band
    return (lower_band, main_band, upper_band)


def append_slab(values, filler, line_axis):
    slab_shape = list(values.shape)
    slab_shape[line_axis] = 1
    return jnp.concatenate([values, jnp.full(slab_shape, filler, values.dtype)], line_axis)


def prepend_slab(values, filler, line_axis):
    slab_shape = list(values.shape)
    slab_shape[line_axis] = 1
    return jnp.concatenate([jnp.full(slab_shape, filler, values.dtype), values], line_axis)


def reduce_solve(lower_band, main_band, upper_band, right_side, line_axis):
    length = right_side.shape[line_axis]
    if length == 1:
        return right_side / main_band
    padded_length = right_side.shape[line_axis]
    half_length = padded_length // 2
    outer_shape = right_side.shape[:line_axis]
    inner_shape = right_side.shape[line_axis + 1 :]

    def paired(values):
        return values.reshape(outer_shape + (half_length, 2) + inner_shape)

    def evens(values):
        return lax.index_in_dim(paired(values), 0, line_axis + 1, keepdims=False)

    def odds(values):
        return lax.index_in_dim(paired(values), 1, line_axis + 1, keepdims=False)

    def following(values, filler):
        return append_slab(
            lax.slice_in_dim(evens(values), 1, half_length, axis=line_axis), filler, line_axis
        )

    left_factor = -odds(lower_band) / evens(main_band)
    right_factor = -odds(upper_band) / following(main_band, 1.0)
    new_lower = left_factor * evens(lower_band)
    new_upper = right_factor * following(upper_band, 0.0)
    new_main = (
        odds(main_band)
        + left_factor * evens(upper_band)
        + right_factor * following(lower_band, 0.0)
    )
    new_right = (
        odds(right_side)
        + left_factor * evens(right_side)
        + right_factor * following(right_side, 0.0)
    )
    odd_values = reduce_solve(new_lower, new_main, new_upper, new_right, line_axis)
    earlier = prepend_slab(
        lax.slice_in_dim(odd_values, 0, half_length - 1, axis=line_axis), 0.0, line_axis
    )
    even_values = (
        evens(right_side) - evens(lower_band) * earlier - evens(upper_band) * odd_values
    ) / evens(main_band)
    joined_shape = list(right_side.shape)
    joined = jnp.stack([even_values, odd_values], line_axis + 1).reshape(joined_shape)
    return joined


def solve_xlines(pieces):
    cond_lines, side_lines = pieces
    lower_band, main_band, upper_band = line_system(cond_lines, 2, inplane_ratio)
    return reduce_solve(lower_band, main_band, upper_band, side_lines, 2)


def solve_ylines(pieces):
    cond_lines, side_lines = pieces
    lower_band, main_band, upper_band = line_system(cond_lines, 1, inplane_ratio)
    return reduce_solve(lower_band, main_band, upper_band, side_lines, 1)


def across_x(transfer_coefficient_volume, first_boundary_face):
    return solve_xlines(
        (
            lax.all_to_all(
                transfer_coefficient_volume, "col", split_axis=1, concat_axis=2, tiled=True
            ),
            lax.all_to_all(first_boundary_face, "col", split_axis=1, concat_axis=2, tiled=True),
        )
    )


def local(
    initial_kelvin_state,
    substance_region,
    source_energy,
    substance_transfer_magnitude,
    substance_softening_rate,
):
    transfer_coefficient_volume = transfer_coefficient_array(
        initial_kelvin_state,
        substance_region,
        substance_transfer_magnitude,
        substance_softening_rate,
    )
    plate_pile = jnp.stack([initial_kelvin_state, transfer_coefficient_volume])
    padded = padded_2(plate_pile, (("row", 2), ("col", 3)), 1)
    implicit_pass_first_axis, implicit_pass_second_axis, implicit_pass_third_axis = (
        forward_diffusion_parts(padded[0], padded[1])
    )
    first_boundary_face = (
        initial_kelvin_state
        + 0.5 * implicit_pass_first_axis
        + implicit_pass_second_axis
        + implicit_pass_third_axis
        + source_energy
    )
    half_along_y = 0.5 * implicit_pass_second_axis
    half_step = across_x(transfer_coefficient_volume, first_boundary_face)
    half_home = lax.all_to_all(half_step, "col", split_axis=2, concat_axis=1, tiled=True)
    second_side = half_home - half_along_y
    new_ylines = solve_ylines(
        (
            lax.all_to_all(
                transfer_coefficient_volume, "row", split_axis=0, concat_axis=1, tiled=True
            ),
            lax.all_to_all(second_side, "row", split_axis=0, concat_axis=1, tiled=True),
        )
    )
    return lax.all_to_all(new_ylines, "row", split_axis=1, concat_axis=0, tiled=True)


def solution(mesh):
    in_specs = (P(None, "row", "col"), P(None, "row", "col"), P(None, "row", "col"), P(), P())
    out_specs = P(None, "row", "col")
    return jax.shard_map(local, mesh=mesh, in_specs=in_specs, out_specs=out_specs, check_vma=False)
```

profile of v0, /device:TPU:0, one launch (start us, length us, event | category | flops | bytes accessed | tf_op | source)
XLA Modules:
  0.0 176.1 jit_solution(5035549960087271334)
XLA Ops:
  2.9 5.9 %exponential_multiply_fusion = f32[8,128,128]{2,1,0:T(8,128)} fusion(f32[8,128,128]{2,1,0:T(8,128)} %param.5, s32[8,128,128]{2,1,0:T(8,128)} %param.6, f32[]{:T(128)} %bitcast.6, f32[]{:T(128)} %bitcast.5, f32[]{:T(128)} %bitcast.4, f32[]{:T(128)} %bitcast.3, f32[]{:T(128)} %bitcast.2, f32[]{:T(128)} %bitcast.1), kind=kLoop, calls=%fused_computation.114 | loop fusion | flops 1179648 | bytes 1572888 | tf_op jit(solution)/shard_map/mul | solution.py:42
  9.6 4.8 %collective-permute-start = (f32[2,8,1,128]{3,2,1,0:T(1,128)S(1)}, f32[2,8,1,128]{3,2,1,0:T(1,128)S(1)}, u32[]{:S(2)}, u32[]{:S(2)}) collective-permute-start(f32[2,8,1,128]{3,2,1,0:T(1,128)S(1)} %get-tuple-element.34), channel_id=1, source_target_pairs={{0,8},{8,16},{16,24},{1,9},{9,17},{17,25},{2,10},{10,18},{18,26},{... | collective-permute-start | bytes 24584 | tf_op jit(solution)/shard_map/ppermute | solution.py:18
  15.7 4.9 %all-to-all-start.4 = ((f32[8,128,128]{2,1,0:T(8,128)}), f32[8,128,128]{2,1,0:T(8,128)S(1)}, u32[]{:S(2)}, u32[]{:S(2)}) async-start(f32[8,128,128]{2,1,0:T(8,128)} %exponential_multiply_fusion), calls=%async_computation.4 | async-start | bytes 1048576 | tf_op jit(solution)/shard_map/all_to_all | solution.py:206
  26.0 2.1 %copy.662 = f32[8,128,128]{2,0,1:T(8,128)} copy(f32[8,128,128]{2,1,0:T(8,128)} %exponential_multiply_fusion) | data formatting | bytes 1048576 | tf_op jit(solution)/shard_map/mul | solution.py:42
  31.0 2.7 %pad_maximum_fusion.1 = f32[2,8,130,130]{3,2,1,0:T(8,128)S(1)} fusion(f32[2,8,130,1]{3,2,1,0:T(8,128)} %copy.659, f32[2,8,1,128]{3,2,1,0:T(1,128)S(1)} %collective-permute-done.1, f32[1,8,128,128]{3,2,1,0:T(8,128)} %bitcast.7, f32[1,8,128,128]{3,2,1,0:T(8,128)S(1)} %bitcast.1349, f32[2,8,1,128]{3,2,1,0:T(1,128)S(1)} %collective-permute-done, ...), kind=kLoop, calls=%fused_computation.1 | loop fusion | flops 1352000 | bytes 2163200 | tf_op jit(solution)/shard_map/concatenate | solution.py:16
  33.8 7.9 %all-to-all-start.1 = ((f32[8,128,128]{2,0,1:T(8,128)}), f32[8,128,128]{2,0,1:T(8,128)}, u32[]{:S(2)}, u32[]{:S(2)}) async-start(f32[8,128,128]{2,0,1:T(8,128)} %copy.662), calls=%async_computation.1 | async-start | bytes 1048576 | tf_op jit(solution)/shard_map/all_to_all | solution.py:167
  42.9 2.2 %fusion.22 = (f32[8,128,128]{2,1,0:T(8,128)S(1)}, f32[8,128,128]{2,1,0:T(8,128)}) fusion(f32[8,128,128]{2,1,0:T(8,128)S(1)} %copy-done.14, f32[8,128,128]{2,1,0:T(8,128)S(1)} %slice.1217, f32[8,128,128]{2,1,0:T(8,128)S(1)} %copy-done.5, f32[8,130,130]{2,1,0:T(8,128)S(1)} %get-tuple-element.26, f32[8,128,128]{2,1,0:T(8,128)S(1)} %slice.1213, ...), kind=kLoop, calls=%fused_computation.61 | loop fusion | flops 5898240 | bytes 8388640 | tf_op jit(solution)/shard_map/add | solution.py:194
  47.0 10.1 %all-to-all-done.1 = f32[8,128,128]{2,0,1:T(8,128)} async-done(((f32[8,128,128]{2,0,1:T(8,128)}), f32[8,128,128]{2,0,1:T(8,128)}, u32[]{:S(2)}, u32[]{:S(2)}) %all-to-all-start.1) | async-done | bytes 524320 | tf_op jit(solution)/shard_map/all_to_all | solution.py:167
  57.1 4.3 %all-to-all-start = ((f32[8,128,128]{2,0,1:T(8,128)}), f32[8,128,128]{2,0,1:T(8,128)}, u32[]{:S(2)}, u32[]{:S(2)}) async-start(f32[8,128,128]{2,0,1:T(8,128)} %copy.660), calls=%async_computation | async-start | bytes 1048576 | tf_op jit(solution)/shard_map/all_to_all | solution.py:170
  63.2 2.7 %copy.668 = f32[8,16,1024]{1,0,2:T(8,128)} copy(f32[8,16,1024]{2,1,0:T(8,128)S(1)} %get-tuple-element.11) | data formatting | bytes 1048576 | tf_op jit(solution)/shard_map/sub | solution.py:87
  69.1 2.7 %copy.664 = f32[8,16,1024]{1,0,2:T(8,128)} copy(f32[8,16,1024]{2,1,0:T(8,128)S(1)} %get-tuple-element.12) | data formatting | bytes 1048576 | tf_op jit(solution)/shard_map/mul | solution.py:85
  75.0 2.7 %copy.671 = f32[8,16,1024]{1,0,2:T(8,128)} copy(f32[8,16,1024]{2,1,0:T(8,128)S(1)} %get-tuple-element.13) | data formatting | bytes 1048576 | tf_op jit(solution)/shard_map/mul | solution.py:86
  81.1 2.5 %bitcast_multiply_fusion = f32[8,16,512,1]{1,0,2,3:T(8,128)S(1)} fusion(f32[8,16,512,2]{1,0,3,2:T(8,128)S(1)} %bitcast.1314, f32[8,16,512,2]{1,0,3,2:T(8,128)} %bitcast.1318), kind=kLoop, calls=%fused_computation.17 | loop fusion | flops 196608 | bytes 1048576 | tf_op jit(solution)/shard_map/mul | solution.py:128
  83.7 3.9 %copy.661 = f32[8,8,16,128]{2,0,3,1:T(8,128)} copy(f32[8,8,16,128]{3,0,2,1:T(8,128)} %bitcast.10) | data formatting | bytes 1048576 | tf_op jit(solution)/shard_map/all_to_all | solution.py:170
  91.9 5.5 %fusion.7 = (f32[8,16,512]{1,0,2:T(8,128)S(1)}, f32[8,16,512]{1,0,2:T(8,128)S(1)}, f32[8,16,512]{1,0,2:T(8,128)S(1)}) fusion(f32[8,16,512,2]{1,0,3,2:T(8,128)} %bitcast.1325, f32[8,16,511]{1,0,2:T(8,128)S(1)} %slice.1231, f32[8,16,512,2]{1,0,3,2:T(8,128)S(1)} %bitcast.1315, f32[8,16,512,2]{1,0,3,2:T(8,128)} %bitcast.1319, f32[8,16,511]{1,0,2:T(8,128)S(1)} %copy-done.6, ...), kind=kLoop, calls=%fused_computation.14 | loop fusion | flops 851968 | bytes 3667968 | tf_op jit(solution)/shard_map/add | solution.py:136
  111.9 2.4 %copy.752 = f32[8,16,512,2]{1,0,3,2:T(8,128)} copy(f32[8,16,512,2]{1,0,2,3:T(8,128)S(1)} %pad_maximum_fusion) | data formatting | bytes 1048576 | tf_op jit(solution)/shard_map/stack | solution.py:148
  114.2 4.4 %reshape.829 = f32[8,1,16384]{2,1,0:T(1,128)} reshape(f32[1024,8,16]{2,1,0:T(8,128)} %bitcast.1344) | data formatting | bytes 1048576
  118.7 4.8 %all-to-all-start.2 = ((f32[8,1,16384]{2,1,0:T(1,128)}), f32[8,1,16384]{2,1,0:T(1,128)S(1)}, u32[]{:S(2)}, u32[]{:S(2)}) async-start(f32[8,1,16384]{2,1,0:T(1,128)} %reshape.829), calls=%async_computation.2 | async-start | bytes 1048576 | tf_op jit(solution)/shard_map/all_to_all | solution.py:202
  125.1 13.7 %all-to-all-done.2 = f32[8,1,16384]{2,1,0:T(1,128)S(1)} async-done(((f32[8,1,16384]{2,1,0:T(1,128)}), f32[8,1,16384]{2,1,0:T(1,128)S(1)}, u32[]{:S(2)}, u32[]{:S(2)}) %all-to-all-start.2) | async-done | bytes 524320 | tf_op jit(solution)/shard_map/all_to_all | solution.py:202
  141.2 3.4 %reshape.830 = f32[1024,8,16]{2,1,0:T(8,128)} reshape(f32[8,16384]{1,0:T(8,128)S(1)} %reduce) | data formatting | bytes 1048576
  144.7 2.8 %copy.754 = f32[8,8,16,128]{3,2,1,0:T(8,128)S(1)} copy(f32[8,8,16,128]{2,0,3,1:T(8,128)} %bitcast.1343) | data formatting | bytes 1048576 | tf_op jit(solution)/shard_map/all_to_all | solution.py:202
  148.4 4.2 %all-to-all-start.3 = ((f32[8,128,128]{2,1,0:T(8,128)}), f32[8,128,128]{2,1,0:T(8,128)S(1)}, u32[]{:S(2)}, u32[]{:S(2)}) async-start(f32[8,128,128]{2,1,0:T(8,128)} %bitcast_subtract_fusion), calls=%async_computation.3 | async-start | bytes 1048576 | tf_op jit(solution)/shard_map/all_to_all | solution.py:209
  152.9 7.5 %all-to-all-done.3 = f32[8,128,128]{2,1,0:T(8,128)S(1)} async-done(((f32[8,128,128]{2,1,0:T(8,128)}), f32[8,128,128]{2,1,0:T(8,128)S(1)}, u32[]{:S(2)}, u32[]{:S(2)}) %all-to-all-start.3) | async-done | bytes 524320 | tf_op jit(solution)/shard_map/all_to_all | solution.py:209
  165.3 9.8 %all_to_all.102 = f32[2,512,128]{2,0,1:T(2,128)S(1)} all-to-all(f32[2,512,128]{2,0,1:T(2,128)S(1)} %copy.828), channel_id=1, replica_groups=mesh['row'=4,'col'=8] {'row'}, dimensions={1} | all-to-all | bytes 1048576 | tf_op jit(solution)/shard_map/all_to_all | solution.py:212
  (301 shorter events, 56.0 us)
Async XLA Ops:
  0.0 20.6 %copy-start.5 = (f32[8,128,128]{2,1,0:T(8,128)S(1)}, f32[8,128,128]{2,1,0:T(8,128)}, u32[]{:S(2)}) copy-start(f32[8,128,128]{2,1,0:T(8,128)} %param.5) | copy-start | bytes 1572868
  9.6 11.0 %collective-permute-start = (f32[2,8,1,128]{3,2,1,0:T(1,128)S(1)}, f32[2,8,1,128]{3,2,1,0:T(1,128)S(1)}, u32[]{:S(2)}, u32[]{:S(2)}) collective-permute-start(f32[2,8,1,128]{3,2,1,0:T(1,128)S(1)} %get-tuple-element.34), channel_id=1, source_target_pairs={{0,8},{8,16},{16,24},{1,9},{9,17},{17,25},{2,10},{10,18},{18,26},{... | collective-permute-start | bytes 24584 | tf_op jit(solution)/shard_map/ppermute | solution.py:18
  14.4 6.2 %collective-permute-start.1 = (f32[2,8,1,128]{3,2,1,0:T(1,128)S(1)}, f32[2,8,1,128]{3,2,1,0:T(1,128)S(1)}, u32[]{:S(2)}, u32[]{:S(2)}) collective-permute-start(f32[2,8,1,128]{3,2,1,0:T(1,128)S(1)} %get-tuple-element.35), channel_id=1, source_target_pairs={{8,0},{16,8},{24,16},{9,1},{17,9},{25,17},{10,2},{18,10},{26,18},{... | collective-permute-start | bytes 24584 | tf_op jit(solution)/shard_map/ppermute | solution.py:20
  15.7 18.0 %all-to-all-start.4 = ((f32[8,128,128]{2,1,0:T(8,128)}), f32[8,128,128]{2,1,0:T(8,128)S(1)}, u32[]{:S(2)}, u32[]{:S(2)}) async-start(f32[8,128,128]{2,1,0:T(8,128)} %exponential_multiply_fusion), calls=%async_computation.4 | async-start | bytes 1048576 | tf_op jit(solution)/shard_map/all_to_all | solution.py:206
  22.8 5.4 %collective-permute-start.2 = (f32[2,8,130,1]{2,1,3,0:T(8,128)S(1)}, f32[2,8,130,1]{2,1,3,0:T(8,128)S(1)}, u32[]{:S(2)}, u32[]{:S(2)}) collective-permute-start(f32[2,8,130,1]{2,1,3,0:T(8,128)S(1)} %copy.656), channel_id=1, source_target_pairs={{0,1},{1,2},{2,3},{3,4},{4,5},{5,6},{6,7},{8,9},{9,10},{10,11},{11... | collective-permute-start | bytes 24968 | tf_op jit(solution)/shard_map/ppermute | solution.py:18
  24.7 4.9 %collective-permute-start.3 = (f32[2,8,130,1]{2,1,3,0:T(8,128)S(1)}, f32[2,8,130,1]{2,1,3,0:T(8,128)S(1)}, u32[]{:S(2)}, u32[]{:S(2)}) collective-permute-start(f32[2,8,130,1]{2,1,3,0:T(8,128)S(1)} %copy.657), channel_id=1, source_target_pairs={{1,0},{2,1},{3,2},{4,3},{5,4},{6,5},{7,6},{9,8},{10,9},{11,10},{12... | collective-permute-start | bytes 24968 | tf_op jit(solution)/shard_map/ppermute | solution.py:20
  33.8 23.3 %all-to-all-start.1 = ((f32[8,128,128]{2,0,1:T(8,128)}), f32[8,128,128]{2,0,1:T(8,128)}, u32[]{:S(2)}, u32[]{:S(2)}) async-start(f32[8,128,128]{2,0,1:T(8,128)} %copy.662), calls=%async_computation.1 | async-start | bytes 1048576 | tf_op jit(solution)/shard_map/all_to_all | solution.py:167
  41.8 1.0 copy-start.14
  57.1 26.6 %all-to-all-start = ((f32[8,128,128]{2,0,1:T(8,128)}), f32[8,128,128]{2,0,1:T(8,128)}, u32[]{:S(2)}, u32[]{:S(2)}) async-start(f32[8,128,128]{2,0,1:T(8,128)} %copy.660), calls=%async_computation | async-start | bytes 1048576 | tf_op jit(solution)/shard_map/all_to_all | solution.py:170
  77.7 3.4 %copy-start = (f32[8,16,1024]{1,0,2:T(8,128)S(1)}, f32[8,16,1024]{1,0,2:T(8,128)}, u32[]{:S(2)}) copy-start(f32[8,16,1024]{1,0,2:T(8,128)} %copy.668) | copy-start | bytes 1572868
  83.7 3.9 %copy-start.8 = (f32[8,16,256]{1,0,2:T(8,128)}, f32[8,16,256]{1,0,2:T(8,128)S(1)}, u32[]{:S(2)}) copy-start(f32[8,16,256]{1,0,2:T(8,128)S(1)} %slice_bitcast_fusion.17) | copy-start | bytes 393220
  87.6 2.8 %copy-start.1 = (f32[8,16,1024]{1,0,2:T(8,128)S(1)}, f32[8,16,1024]{1,0,2:T(8,128)}, u32[]{:S(2)}) copy-start(f32[8,16,1024]{1,0,2:T(8,128)} %copy.668) | copy-start | bytes 1572868
  89.5 1.8 %copy-start.6 = (f32[8,16,511]{1,0,2:T(8,128)S(1)}, f32[8,16,511]{1,0,2:T(8,128)}, u32[]{:S(2)}) copy-start(f32[8,16,511]{1,0,2:T(8,128)} %slice.1230) | copy-start | bytes 784900
  89.5 2.4 %copy-start.7 = (f32[8,16,511]{1,0,2:T(8,128)S(1)}, f32[8,16,511]{1,0,2:T(8,128)}, u32[]{:S(2)}) copy-start(f32[8,16,511]{1,0,2:T(8,128)} %slice.1238) | copy-start | bytes 784900
  98.6 1.2 slice-start
  98.6 1.5 slice-start.1
  101.1 1.0 slice-start.2
  106.1 2.2 %copy-start.4 = (f32[8,8,16,128]{2,0,3,1:T(8,128)S(1)}, f32[8,8,16,128]{2,0,3,1:T(8,128)}, u32[]{:S(2)}) copy-start(f32[8,8,16,128]{2,0,3,1:T(8,128)} %copy.661) | copy-start | bytes 1572868
  106.5 3.2 %copy-start.3 = (f32[8,16,1024]{1,0,2:T(8,128)S(1)}, f32[8,16,1024]{1,0,2:T(8,128)}, u32[]{:S(2)}) copy-start(f32[8,16,1024]{1,0,2:T(8,128)} %copy.671) | copy-start | bytes 1572868
  106.6 4.3 %copy-start.2 = (f32[8,16,1024]{1,0,2:T(8,128)S(1)}, f32[8,16,1024]{1,0,2:T(8,128)}, u32[]{:S(2)}) copy-start(f32[8,16,1024]{1,0,2:T(8,128)} %copy.664) | copy-start | bytes 1572868
  114.2 9.3 %copy-start.11 = (f32[2,4,128,128]{3,2,1,0:T(8,128)S(1)}, f32[2,4,128,128]{3,2,1,0:T(8,128)}, u32[]{:S(2)}) copy-start(f32[2,4,128,128]{3,2,1,0:T(8,128)} %copy.757) | copy-start | bytes 1572868
  118.7 20.2 %all-to-all-start.2 = ((f32[8,1,16384]{2,1,0:T(1,128)}), f32[8,1,16384]{2,1,0:T(1,128)S(1)}, u32[]{:S(2)}, u32[]{:S(2)}) async-start(f32[8,1,16384]{2,1,0:T(1,128)} %reshape.829), calls=%async_computation.2 | async-start | bytes 1048576 | tf_op jit(solution)/shard_map/all_to_all | solution.py:202
  144.7 2.9 %copy-start.10 = (f32[8,128,128]{2,1,0:T(8,128)S(1)}, f32[8,128,128]{2,1,0:T(8,128)}, u32[]{:S(2)}) copy-start(f32[8,128,128]{2,1,0:T(8,128)} %get-tuple-element.10) | copy-start | bytes 1572868
  148.4 12.0 %all-to-all-start.3 = ((f32[8,128,128]{2,1,0:T(8,128)}), f32[8,128,128]{2,1,0:T(8,128)S(1)}, u32[]{:S(2)}, u32[]{:S(2)}) async-start(f32[8,128,128]{2,1,0:T(8,128)} %bitcast_subtract_fusion), calls=%async_computation.3 | async-start | bytes 1048576 | tf_op jit(solution)/shard_map/all_to_all | solution.py:209
  (4 other events, 3.6 us)
where the time goes:
time: 177 us; the launch traced here: 176 us
  local copies, waits for them, and re-layouts  68.9 us (39%)
  starting transfers between devices  34.8 us (20%)
  waiting for transfers between devices  31.4 us (18%)
  other arithmetic  29.2 us (16%)
  blocking collectives  9.85 us (6%)
  between operations  1.93 us (1%)
    unnamed x32, local copies, waits for them, and re-layouts  15.8 us
    all_to_all x1, waiting for transfers between devices, local(): lax.all_to_all(half_step, 'col', split_axis=2, concat_axis=1, tiled=True)  13.7 us
    all_to_all x1, waiting for transfers between devices, across_x(): lax.all_to_all(transfer_coefficient_volume, 'col', split_axis=1, concat_a...  10.1 us
    all_to_all x1, blocking collectives, local(): lax.all_to_all(new_ylines, 'row', split_axis=1, concat_axis=0, tiled=True)  9.85 us
    slice x72, local copies, waits for them, and re-layouts, following(): lax.slice_in_dim(evens(values), 1, half_length, axis=line_axis)  8.24 us
    all_to_all x1, starting transfers between devices, across_x(): lax.all_to_all(transfer_coefficient_volume, 'col', split_axis=1, concat_a...  7.87 us
    squeeze x36, local copies, waits for them, and re-layouts, evens(): return lax.index_in_dim(paired(values), 0, line_axis + 1, keepdims=False)  7.81 us
    add x15, other arithmetic, reduce_solve(): odds(right_side) + left_factor * evens(right_side)  7.57 us
  transfers between devices with their start and end apart: 9, of which 3 were waited for; matrix products, arithmetic and copies ran while one was open for 22% of the time, Pallas kernels for 0%

commit v1 on v0

v1 whole, which is shorter than its diff:
```python
import functools

import jax
import jax.numpy as jnp
from jax import lax
from jax.experimental import pallas as pl
from jax.experimental.pallas import tpu as pltpu
from jax.sharding import PartitionSpec as P

MESH = pl.DeviceIdType.MESH
inplane_half = 500.0
depth_ratio = 0.08

NZ = 8
L = 128
BLOCK = 16


def inverse(value):
    guess = pl.reciprocal(value, approx=True)
    return guess * (2.0 - value * guess)


def pairs(values):
    split = values.reshape((values.shape[0] // 2, 2) + values.shape[1:])
    return split[:, 0], split[:, 1]


def shifted_up(values, last):
    if values.shape[0] == 1:
        return last
    return jnp.concatenate([values[1:], last], axis=0)


def shifted_down(values, first):
    if values.shape[0] == 1:
        return first
    return jnp.concatenate([first, values[:-1]], axis=0)


def nodes(ref, first, count):
    return ref[pl.ds(first * NZ, count * NZ), :].reshape(count, NZ, L)


def put_nodes(ref, first, values):
    count = values.shape[0]
    ref[pl.ds(first * NZ, count * NZ), :] = values.reshape(count * NZ, L)


def levels():
    count = L
    while count > 1:
        half = count // 2
        yield count, half, L - 2 * count, L - 2 * half
        count = half


def eliminate_coefficients(link_ref, gl_ref, gr_ref, r_ref, w_ref, s_ref):
    pushed_out = jnp.zeros((1, NZ, L), jnp.float32)
    for count, half, node_at, pair_at in levels():
        block = min(half, BLOCK)
        carry = jnp.zeros((1, NZ, L), jnp.float32)
        for first in reversed(range(0, half, block)):
            if count == L:
                wl, wr = pairs(nodes(link_ref, 2 * first, 2 * block))
                inv = inverse(1.0 + wl + wr)
                gl, gr = wl * inv, wr * inv
                push = gl
                surplus = 1.0 + gr + shifted_up(push, carry)
            else:
                wl, wr = pairs(nodes(w_ref, node_at + 2 * first, 2 * block))
                se, so = pairs(nodes(s_ref, node_at + 2 * first, 2 * block))
                inv = inverse(se + wl + wr)
                gl, gr = wl * inv, wr * inv
                push = gl * se
                surplus = so + gr * se + shifted_up(push, carry)
            carry = push[:1]
            put_nodes(gl_ref, pair_at + first, gl)
            put_nodes(gr_ref, pair_at + first, gr)
            put_nodes(r_ref, pair_at + first, inv)
            put_nodes(w_ref, L - 2 * half + first, gl * wr)
            put_nodes(s_ref, L - 2 * half + first, surplus)
        pushed_out = pushed_out + carry
    return w_ref[pl.ds((L - 2) * NZ, NZ), :], s_ref[pl.ds((L - 2) * NZ, NZ), :], pushed_out[0]


def eliminate_right_side(side_ref, gl_ref, gr_ref, r_ref, d_ref, q_ref):
    pushed_out = jnp.zeros((1, NZ, L), jnp.float32)
    for count, half, node_at, pair_at in levels():
        block = min(half, BLOCK)
        carry = jnp.zeros((1, NZ, L), jnp.float32)
        for first in reversed(range(0, half, block)):
            if count == L:
                de, do = pairs(nodes(side_ref, 2 * first, 2 * block))
            else:
                de, do = pairs(nodes(d_ref, node_at + 2 * first, 2 * block))
            push = nodes(gl_ref, pair_at + first, block) * de
            side = do + nodes(gr_ref, pair_at + first, block) * de + shifted_up(push, carry)
            carry = push[:1]
            put_nodes(q_ref, pair_at + first, nodes(r_ref, pair_at + first, block) * de)
            put_nodes(d_ref, L - 2 * half + first, side)
        pushed_out = pushed_out + carry
    return d_ref[pl.ds((L - 2) * NZ, NZ), :], pushed_out[0]


def substitute(before, last, gl_ref, gr_ref, q_ref, v_ref, store):
    v_ref[pl.ds((L - 2) * NZ, NZ), :] = last
    for count, half, node_at, pair_at in reversed(list(levels())):
        block = min(half, BLOCK)
        carry = before[None]
        for first in range(0, half, block):
            vo = nodes(v_ref, L - 2 * half + first, block)
            ve = (
                nodes(gl_ref, pair_at + first, block) * shifted_down(vo, carry)
                + nodes(gr_ref, pair_at + first, block) * vo
                + nodes(q_ref, pair_at + first, block)
            )
            carry = vo[block - 1 :]
            joined = jnp.stack([ve, vo], axis=1).reshape(2 * block, NZ, L)
            if count == L:
                store(2 * first, joined)
            else:
                put_nodes(v_ref, node_at + 2 * first, joined)


def factor_chain(n, coefficients, chain_g, chain_r):
    flow = None
    for p in range(n):
        surplus = coefficients[p, NZ : 2 * NZ, :]
        if p < n - 1:
            surplus = surplus + coefficients[p + 1, 2 * NZ :, :]
        if flow is not None:
            surplus = surplus + flow
        if p < n - 1:
            weight = coefficients[p + 1, :NZ, :]
            inv = inverse(surplus + weight)
            share = weight * inv
            chain_g[p] = share
            flow = share * surplus
        else:
            inv = inverse(surplus)
        chain_r[p] = inv


def solve_chain(n, sides, chain_g, chain_r, chain_v):
    flow = None
    scaled = []
    for p in range(n):
        side = sides[p, :NZ, :]
        if p < n - 1:
            side = side + sides[p + 1, NZ:, :]
        if flow is not None:
            side = side + flow
        if p < n - 1:
            flow = chain_g[p] * side
        scaled.append(side * chain_r[p])
    value = scaled[n - 1]
    chain_v[0] = jnp.zeros((NZ, L), jnp.float32)
    chain_v[n] = value
    for p in reversed(range(n - 1)):
        value = scaled[p] + chain_g[p] * value
        chain_v[p + 1] = value


class Gather:
    def __init__(self, axis, n, buffer, send, recv):
        self.axis, self.n, self.buffer, self.send, self.recv = axis, n, buffer, send, recv
        self.me = lax.axis_index(axis)

    def copy(self, step, slot):
        return pltpu.make_async_remote_copy(
            src_ref=self.buffer.at[slot],
            dst_ref=self.buffer.at[slot],
            send_sem=self.send.at[step - 1],
            recv_sem=self.recv.at[step - 1],
            device_id={self.axis: lax.rem(self.me + step, self.n)},
            device_id_type=MESH,
        )

    def start(self):
        for step in range(1, self.n):
            self.copy(step, self.me).start()

    def wait(self):
        for step in range(1, self.n):
            self.copy(step, lax.rem(self.me + self.n - step, self.n)).wait_recv()

    def finish(self):
        for step in range(1, self.n):
            self.copy(step, self.me).wait_send()


class Halo:
    def __init__(self, axis, n, edges, halo, send, recv):
        self.axis, self.n, self.edges, self.halo, self.send, self.recv = axis, n, edges, halo, send, recv
        self.me = lax.axis_index(axis)

    def copy(self, side):
        to = self.me - 1 if side == 0 else self.me + 1
        return pltpu.make_async_remote_copy(
            src_ref=self.edges.at[side],
            dst_ref=self.halo.at[1 - side],
            send_sem=self.send.at[side],
            recv_sem=self.recv.at[1 - side],
            device_id={self.axis: to},
            device_id_type=MESH,
        )

    def start(self):
        @pl.when(self.me > 0)
        def _():
            self.copy(0).start()

        @pl.when(self.me < self.n - 1)
        def _():
            self.copy(1).start()

    def wait(self):
        @pl.when(self.me > 0)
        def _():
            self.copy(1).wait_recv()

        @pl.when(self.me == 0)
        def _():
            self.halo[0] = jnp.zeros((2 * NZ, L), jnp.float32)

        @pl.when(self.me < self.n - 1)
        def _():
            self.copy(0).wait_recv()

        @pl.when(self.me == self.n - 1)
        def _():
            self.halo[1] = jnp.zeros((2 * NZ, L), jnp.float32)

    def finish(self):
        @pl.when(self.me > 0)
        def _():
            self.copy(0).wait_send()

        @pl.when(self.me < self.n - 1)
        def _():
            self.copy(1).wait_send()


def links(cond, field, cond_before, field_before):
    beside = shifted_down(cond, cond_before)
    weight = (2.0 * inplane_half) * cond * beside * inverse(cond + beside)
    return weight, weight * (field - shifted_down(field, field_before))


def kernel(
    n_row,
    n_col,
    mag,
    rate,
    field_hbm,
    region_hbm,
    source_hbm,
    out_hbm,
    field,
    region,
    source,
    cond,
    base,
    half_y,
    link_y,
    field_x,
    cond_x,
    side_x,
    link_x,
    solved,
    out,
    gl_x,
    gr_x,
    r_x,
    gl_y,
    gr_y,
    r_y,
    work_a,
    work_b,
    edges_y,
    halo_y,
    edges_x,
    halo_x,
    coef_x,
    rhs_x,
    coef_y,
    rhs_y,
    chain_gx,
    chain_rx,
    chain_vx,
    chain_gy,
    chain_ry,
    chain_vy,
    in_sem,
    out_sem,
    hy_send,
    hy_recv,
    hx_send,
    hx_recv,
    cx_send,
    cx_recv,
    rx_send,
    rx_recv,
    cy_send,
    cy_recv,
    ry_send,
    ry_recv,
):
    loads = [
        pltpu.make_async_copy(field_hbm, field, in_sem.at[0]),
        pltpu.make_async_copy(region_hbm, region, in_sem.at[1]),
        pltpu.make_async_copy(source_hbm, source, in_sem.at[2]),
    ]
    for load in loads:
        load.start()
    my_row, my_col = lax.axis_index("row"), lax.axis_index("col")
    barrier = pltpu.get_barrier_semaphore()
    for step in range(1, n_row):
        pl.semaphore_signal(
            barrier, inc=1, device_id={"row": lax.rem(my_row + step, n_row)}, device_id_type=MESH
        )
    for step in range(1, n_col):
        pl.semaphore_signal(
            barrier, inc=1, device_id={"col": lax.rem(my_col + step, n_col)}, device_id_type=MESH
        )

    share_y = Halo("row", n_row, edges_y, halo_y, hy_send, hy_recv)
    share_x = Halo("col", n_col, edges_x, halo_x, hx_send, hx_recv)
    gather_cx = Gather("col", n_col, coef_x, cx_send, cx_recv)
    gather_rx = Gather("col", n_col, rhs_x, rx_send, rx_recv)
    gather_cy = Gather("row", n_row, coef_y, cy_send, cy_recv)
    gather_ry = Gather("row", n_row, rhs_y, ry_send, ry_recv)

    m0, m1, m2 = mag[0], mag[1], mag[2]
    k0, k1, k2 = rate[0], rate[1], rate[2]

    def conductivity(kelvin, kind):
        first, second = kind == 0, kind == 1
        scale = jnp.where(first, m0, jnp.where(second, m1, m2))
        soft = jnp.where(first, k0, jnp.where(second, k1, k2))
        return scale * jnp.exp(-soft * kelvin)

    loads[0].wait()
    loads[1].wait()
    for side, y in ((0, 0), (1, L - 1)):
        kelvin = field[pl.ds(y, NZ, stride=L), :]
        edges_y[side, :NZ, :] = kelvin
        edges_y[side, NZ:, :] = conductivity(kelvin, region[pl.ds(y, NZ, stride=L), :])
    pl.semaphore_wait(barrier, n_row + n_col - 2)
    share_y.start()

    for z in range(NZ):
        rows = pl.ds(z * L, L)
        kelvin = field[rows, :]
        value = conductivity(kelvin, region[rows, :])
        cond[rows, :] = value
        field_x[pl.ds(z, L, stride=NZ), :] = kelvin.T
        cond_x[pl.ds(z, L, stride=NZ), :] = value.T
    for side, x in ((0, 0), (1, L - 1)):
        edges_x[side, :NZ, :] = field_x[pl.ds(x * NZ, NZ), :]
        edges_x[side, NZ:, :] = cond_x[pl.ds(x * NZ, NZ), :]
    share_x.start()

    share_y.wait()
    t_before, c_before = halo_y[0, :NZ, :][None], halo_y[0, NZ:, :][None]
    flux_before = None
    for first in range(0, L + 1, BLOCK):
        if first < L:
            t = jnp.stack([field[pl.ds(first + i, NZ, stride=L), :] for i in range(BLOCK)])
            c = jnp.stack([cond[pl.ds(first + i, NZ, stride=L), :] for i in range(BLOCK)])
        else:
            t, c = halo_y[1, :NZ, :][None], halo_y[1, NZ:, :][None]
        weight, flux = links(c, t, c_before, t_before)
        if first < L:
            put_nodes(link_y, first, weight)
            put_nodes(half_y, first, shifted_up(flux, flux[-1:]) - flux)
        if flux_before is not None:
            half_y[pl.ds((first - 1) * NZ, NZ), :] = flux[0] - flux_before
        t_before, c_before, flux_before = t[-1:], c[-1:], flux[-1]
    w, s, push = eliminate_coefficients(link_y, gl_y, gr_y, r_y, work_a, work_b)
    coef_y[my_row, :NZ, :] = w
    coef_y[my_row, NZ : 2 * NZ, :] = s
    coef_y[my_row, 2 * NZ :, :] = push
    gather_cy.start()

    loads[2].wait()
    lower = None
    for z in range(NZ):
        rows = pl.ds(z * L, L)
        t, c = field[rows, :], cond[rows, :]
        if z == 0:
            lower = depth_ratio * c * t
        if z < NZ - 1:
            above = pl.ds((z + 1) * L, L)
            ta, ca = field[above, :], cond[above, :]
            upper = (2.0 * depth_ratio) * c * ca * inverse(c + ca) * (ta - t)
            along_z = upper - lower
            lower = upper
        else:
            along_z = -lower
        total = t + 2.0 * half_y[pl.ds(z, L, stride=NZ), :] + along_z + source[rows, :]
        side_x[pl.ds(z, L, stride=NZ), :] = total.T

    share_x.wait()
    t_before, c_before = halo_x[0, :NZ, :][None], halo_x[0, NZ:, :][None]
    flux_before = None
    for first in range(0, L + 1, BLOCK):
        if first < L:
            t, c = nodes(field_x, first, BLOCK), nodes(cond_x, first, BLOCK)
        else:
            t, c = halo_x[1, :NZ, :][None], halo_x[1, NZ:, :][None]
        weight, flux = links(c, t, c_before, t_before)
        if first < L:
            put_nodes(link_x, first, weight)
            extra = shifted_up(flux, jnp.zeros((1, NZ, L), jnp.float32)) - flux
            put_nodes(side_x, first, nodes(side_x, first, BLOCK) + extra)
        if first > 0:
            at = pl.ds((first - 1) * NZ, NZ)
            side_x[at, :] = side_x[at, :] + flux[0]
        t_before, c_before = t[-1:], c[-1:]
    w, s, push = eliminate_coefficients(link_x, gl_x, gr_x, r_x, work_a, work_b)
    coef_x[my_col, :NZ, :] = w
    coef_x[my_col, NZ : 2 * NZ, :] = s
    coef_x[my_col, 2 * NZ :, :] = push
    gather_cx.start()
    d, push = eliminate_right_side(side_x, gl_x, gr_x, r_x, work_a, work_b)
    rhs_x[my_col, :NZ, :] = d
    rhs_x[my_col, NZ:, :] = push
    gather_rx.start()

    gather_cy.wait()
    factor_chain(n_row, coef_y, chain_gy, chain_ry)
    gather_cx.wait()
    factor_chain(n_col, coef_x, chain_gx, chain_rx)
    gather_rx.wait()
    solve_chain(n_col, rhs_x, chain_gx, chain_rx, chain_vx)

    def store_x(first, values):
        put_nodes(solved, first, values)

    substitute(chain_vx[my_col], chain_vx[my_col + 1], gl_x, gr_x, work_b, work_a, store_x)

    for z in range(NZ):
        at = pl.ds(z, L, stride=NZ)
        side_x[at, :] = solved[at, :].T - half_y[at, :]
    d, push = eliminate_right_side(side_x, gl_y, gr_y, r_y, work_a, work_b)
    rhs_y[my_row, :NZ, :] = d
    rhs_y[my_row, NZ:, :] = push
    gather_ry.start()
    gather_ry.wait()
    solve_chain(n_row, rhs_y, chain_gy, chain_ry, chain_vy)

    def store_y(first, values):
        for i in range(values.shape[0]):
            out[pl.ds(first + i, NZ, stride=L), :] = values[i]

    substitute(chain_vy[my_row], chain_vy[my_row + 1], gl_y, gr_y, work_b, work_a, store_y)
    result = pltpu.make_async_copy(out, out_hbm, out_sem)
    result.start()
    for transfer in (share_y, share_x, gather_cx, gather_rx, gather_cy, gather_ry):
        transfer.finish()
    result.wait()


def solution(mesh):
    n_row, n_col = mesh.shape["row"], mesh.shape["col"]

    def local(field, region, source, mag, rate):
        def flat(values):
            return values.reshape(NZ * L, L)

        whole = pltpu.VMEM((NZ * L, L), jnp.float32)
        integer = pltpu.VMEM((NZ * L, L), jnp.int32)

        def stack(count, height):
            return pltpu.VMEM((count, height * NZ, L), jnp.float32)

        def dma(count):
            return pltpu.SemaphoreType.DMA((count,))

        result = pl.pallas_call(
            functools.partial(kernel, n_row, n_col),
            out_shape=jax.ShapeDtypeStruct((NZ * L, L), jnp.float32),
            in_specs=[pl.BlockSpec(memory_space=pltpu.SMEM)] * 2 + [pl.BlockSpec(memory_space=pl.ANY)] * 3,
            out_specs=pl.BlockSpec(memory_space=pl.ANY),
            scratch_shapes=[whole, integer]
            + [whole] * 19
            + [stack(2, 2)] * 4
            + [stack(n_col, 3), stack(n_col, 2), stack(n_row, 3), stack(n_row, 2)]
            + [stack(n_col, 1), stack(n_col, 1), stack(n_col + 1, 1)]
            + [stack(n_row, 1), stack(n_row, 1), stack(n_row + 1, 1)]
            + [dma(3), pltpu.SemaphoreType.DMA]
            + [dma(2)] * 4
            + [dma(n_col - 1)] * 4
            + [dma(n_row - 1)] * 4,
            compiler_params=pltpu.CompilerParams(
                collective_id=0, has_side_effects=True, vmem_limit_bytes=40 * 1024 * 1024
            ),
            cost_estimate=pl.CostEstimate(
                flops=20_000_000, bytes_accessed=2_200_000, transcendentals=400_000
            ),
        )(mag, rate, flat(field), flat(region), flat(source))
        return result.reshape(NZ, L, L)

    spec = P(None, "row", "col")
    return jax.shard_map(
        local, mesh=mesh, in_specs=(spec, spec, spec, P(), P()), out_specs=spec, check_vma=False
    )
```

time: 177 us -> 24.2 us (0.14)
  local copies, waits for them, and re-layouts: 68.9 us -> 4.59 us
  starting transfers between devices: 34.8 us -> 0 us
  waiting for transfers between devices: 31.4 us -> 0 us
  other arithmetic: 29.2 us -> 0 us
  Pallas kernels: 0 us -> 19.3 us
  blocking collectives: 9.85 us -> 0 us
  between operations: 1.93 us -> 0.01 us
    all_to_all x5 -> x0, waiting for transfers between devices: 31.4 us -> none  [the longest x1 13.7 us: local(): lax.all_to_all(half_step, 'col', split_axis=2, concat_axis=1, tiled=True)]
    all_to_all x5 -> x0, starting transfers between devices: 26.1 us -> none  [the longest x1 7.87 us: across_x(): lax.all_to_all(transfer_coefficient_volume, 'col', split_axis=1, concat_a...]
    pallas_call x0 -> x1, Pallas kernels: none -> 19.3 us  [local(): pl.pallas_call(functools.partial(kernel, n_row, n_col), out_shape=jax.Sha...]
    slice x121 -> x0, local copies, waits for them, and re-layouts: 16.6 us -> none  [the longest x72 8.24 us: following(): lax.slice_in_dim(evens(values), 1, half_length, axis=line_axis)]
    unnamed x32 -> x11, local copies, waits for them, and re-layouts: 15.8 us -> 4.59 us
    all_to_all x9 -> x0, local copies, waits for them, and re-layouts: 10.4 us -> none  [the longest x1 3.85 us: across_x(): lax.all_to_all(first_boundary_face, 'col', split_axis=1, concat_axis=2, t...]
    all_to_all x1 -> x0, blocking collectives: 9.85 us -> none  [local(): lax.all_to_all(new_ylines, 'row', split_axis=1, concat_axis=0, tiled=True)]
    add x16 -> x0, other arithmetic: 9.74 us -> none  [the longest x15 7.57 us: reduce_solve(): odds(right_side) + left_factor * evens(right_side)]
  transfers between devices with their start and end apart: 9 -> 0, of which waited for: 3 -> 0; matrix products, arithmetic and copies ran while one was open for 22% -> 0% of each run, Pallas kernels for 0% -> 0%
where the time goes in v1:
time: 24.2 us; the launch traced here: 23.9 us
  Pallas kernels  19.3 us (80%)
  local copies, waits for them, and re-layouts  4.59 us (19%)
    pallas_call x1, Pallas kernels, local(): pl.pallas_call(functools.partial(kernel, n_row, n_col), out_shape=jax.Sha...  19.3 us
    unnamed x11, local copies, waits for them, and re-layouts  4.59 us

profile of v1, /device:TPU:0, one launch (start us, length us, event | category | flops | bytes accessed | tf_op | source)
XLA Modules:
  0.0 23.9 jit_solution(18041690291731499385)
XLA Ops:
  0.0 0.0 copy-start.3
  0.0 0.0 copy-start.4
  0.0 0.7 %copy-done.3 = f32[3]{0:T(128)S(1)} copy-done((f32[3]{0:T(128)S(1)}, f32[3]{0:T(128)}, u32[]{:S(2)}) %copy-start.3) | copy-done | bytes 36
  0.7 0.0 copy-done.4
  0.7 0.0 copy-start
  0.7 1.0 %copy-done = f32[8,128,128]{2,1,0:T(8,128)S(1)} copy-done((f32[8,128,128]{2,1,0:T(8,128)S(1)}, f32[8,128,128]{2,1,0:T(8,128)}, u32[]{:S(2)}) %copy-start) | copy-done | bytes 524312
  1.7 0.0 copy-start.1
  1.7 1.0 %copy-done.1 = s32[8,128,128]{2,1,0:T(8,128)S(1)} copy-done((s32[8,128,128]{2,1,0:T(8,128)S(1)}, s32[8,128,128]{2,1,0:T(8,128)}, u32[]{:S(2)}) %copy-start.1) | copy-done | bytes 524312
  2.8 0.0 copy-start.2
  2.8 1.0 %copy-done.2 = f32[8,128,128]{2,1,0:T(8,128)S(1)} copy-done((f32[8,128,128]{2,1,0:T(8,128)S(1)}, f32[8,128,128]{2,1,0:T(8,128)}, u32[]{:S(2)}) %copy-start.2) | copy-done | bytes 524312
  3.8 19.3 %shard_map.55 = f32[1024,128]{1,0:T(8,128)S(1)} custom-call(f32[3]{0:T(128)S(1)} %copy-done.3, f32[3]{0:T(128)S(1)} %copy-done.4, f32[1024,128]{1,0:T(8,128)S(1)} %bitcast.5, s32[1024,128]{1,0:T(8,128)S(1)} %bitcast.6, f32[1024,128]{1,0:T(8,128)S(1)} %bitcast.7), custom_call_target="tpu_custom_call" | custom-call | flops 20000000 | bytes 2200000 | tf_op jit(solution)/shard_map/pallas_call | solution.py:482
  23.1 0.8 %copy.7 = f32[8,128,128]{2,1,0:T(8,128)} copy(f32[8,128,128]{2,1,0:T(8,128)S(1)} %bitcast.4) | data formatting | bytes 1048576
Async XLA Ops:
  0.0 0.7 %copy-start.3 = (f32[3]{0:T(128)S(1)}, f32[3]{0:T(128)}, u32[]{:S(2)}) copy-start(f32[3]{0:T(128)} %mag.1) | copy-start | bytes 40
  0.0 0.7 %copy-start.4 = (f32[3]{0:T(128)S(1)}, f32[3]{0:T(128)}, u32[]{:S(2)}) copy-start(f32[3]{0:T(128)} %rate.1) | copy-start | bytes 40
  0.7 1.0 %copy-start = (f32[8,128,128]{2,1,0:T(8,128)S(1)}, f32[8,128,128]{2,1,0:T(8,128)}, u32[]{:S(2)}) copy-start(f32[8,128,128]{2,1,0:T(8,128)} %param.5) | copy-start | bytes 1572868
  1.7 1.0 %copy-start.1 = (s32[8,128,128]{2,1,0:T(8,128)S(1)}, s32[8,128,128]{2,1,0:T(8,128)}, u32[]{:S(2)}) copy-start(s32[8,128,128]{2,1,0:T(8,128)} %param.6) | copy-start | bytes 1572868
  2.8 1.0 %copy-start.2 = (f32[8,128,128]{2,1,0:T(8,128)S(1)}, f32[8,128,128]{2,1,0:T(8,128)}, u32[]{:S(2)}) copy-start(f32[8,128,128]{2,1,0:T(8,128)} %param.7) | copy-start | bytes 1572868

commit v2 on v1

--- a/solution.py
+++ b/solution.py
@@ -251,17 +251,18 @@
 def kernel(
     n_row,
     n_col,
-    mag,
-    rate,
+    mag_hbm,
+    rate_hbm,
     field_hbm,
     region_hbm,
     source_hbm,
-    out_hbm,
+    out,
+    mag,
+    rate,
     field,
     region,
     source,
     cond,
-    base,
     half_y,
     link_y,
     field_x,
@@ -269,7 +270,6 @@
     side_x,
     link_x,
     solved,
-    out,
     gl_x,
     gr_x,
     r_x,
@@ -278,6 +278,8 @@
     r_y,
     work_a,
     work_b,
+    work_c,
+    work_d,
     edges_y,
     halo_y,
     edges_x,
@@ -292,8 +294,8 @@
     chain_gy,
     chain_ry,
     chain_vy,
+    par_sem,
     in_sem,
-    out_sem,
     hy_send,
     hy_recv,
     hx_send,
@@ -307,12 +309,25 @@
     ry_send,
     ry_recv,
 ):
+    parameters = [
+        pltpu.make_async_copy(mag_hbm, mag, par_sem.at[0]),
+        pltpu.make_async_copy(rate_hbm, rate, par_sem.at[1]),
+    ]
+    for load in parameters:
+        load.start()
+
+    def layer(source_ref, target_ref, kind, z):
+        rows = pl.ds(z * L, L)
+        return pltpu.make_async_copy(source_ref.at[rows], target_ref.at[rows], in_sem.at[kind, z])
+
     loads = [
-        pltpu.make_async_copy(field_hbm, field, in_sem.at[0]),
-        pltpu.make_async_copy(region_hbm, region, in_sem.at[1]),
-        pltpu.make_async_copy(source_hbm, source, in_sem.at[2]),
+        (layer(field_hbm, field, 0, z), layer(region_hbm, region, 1, z)) for z in range(NZ)
     ]
-    for load in loads:
+    source_loads = [layer(source_hbm, source, 2, z) for z in range(NZ)]
+    for field_load, region_load in loads:
+        field_load.start()
+        region_load.start()
+    for load in source_loads:
         load.start()
     my_row, my_col = lax.axis_index("row"), lax.axis_index("col")
     barrier = pltpu.get_barrier_semaphore()
@@ -332,6 +347,8 @@
     gather_cy = Gather("row", n_row, coef_y, cy_send, cy_recv)
     gather_ry = Gather("row", n_row, rhs_y, ry_send, ry_recv)
 
+    for load in parameters:
+        load.wait()
     m0, m1, m2 = mag[0], mag[1], mag[2]
     k0, k1, k2 = rate[0], rate[1], rate[2]
 
@@ -341,22 +358,21 @@
         soft = jnp.where(first, k0, jnp.where(second, k1, k2))
         return scale * jnp.exp(-soft * kelvin)
 
-    loads[0].wait()
-    loads[1].wait()
+    for z in range(NZ):
+        rows = pl.ds(z * L, L)
+        for load in loads[z]:
+            load.wait()
+        cond[rows, :] = conductivity(field[rows, :], region[rows, :])
     for side, y in ((0, 0), (1, L - 1)):
-        kelvin = field[pl.ds(y, NZ, stride=L), :]
-        edges_y[side, :NZ, :] = kelvin
-        edges_y[side, NZ:, :] = conductivity(kelvin, region[pl.ds(y, NZ, stride=L), :])
+        edges_y[side, :NZ, :] = field[pl.ds(y, NZ, stride=L), :]
+        edges_y[side, NZ:, :] = cond[pl.ds(y, NZ, stride=L), :]
     pl.semaphore_wait(barrier, n_row + n_col - 2)
     share_y.start()
 
     for z in range(NZ):
         rows = pl.ds(z * L, L)
-        kelvin = field[rows, :]
-        value = conductivity(kelvin, region[rows, :])
-        cond[rows, :] = value
-        field_x[pl.ds(z, L, stride=NZ), :] = kelvin.T
-        cond_x[pl.ds(z, L, stride=NZ), :] = value.T
+        field_x[pl.ds(z, L, stride=NZ), :] = field[rows, :].T
+        cond_x[pl.ds(z, L, stride=NZ), :] = cond[rows, :].T
     for side, x in ((0, 0), (1, L - 1)):
         edges_x[side, :NZ, :] = field_x[pl.ds(x * NZ, NZ), :]
         edges_x[side, NZ:, :] = cond_x[pl.ds(x * NZ, NZ), :]
@@ -378,13 +394,9 @@
         if flux_before is not None:
             half_y[pl.ds((first - 1) * NZ, NZ), :] = flux[0] - flux_before
         t_before, c_before, flux_before = t[-1:], c[-1:], flux[-1]
-    w, s, push = eliminate_coefficients(link_y, gl_y, gr_y, r_y, work_a, work_b)
-    coef_y[my_row, :NZ, :] = w
-    coef_y[my_row, NZ : 2 * NZ, :] = s
-    coef_y[my_row, 2 * NZ :, :] = push
-    gather_cy.start()
-
-    loads[2].wait()
+
+    for load in source_loads:
+        load.wait()
     lower = None
     for z in range(NZ):
         rows = pl.ds(z * L, L)
@@ -429,8 +441,11 @@
     rhs_x[my_col, NZ:, :] = push
     gather_rx.start()
 
-    gather_cy.wait()
-    factor_chain(n_row, coef_y, chain_gy, chain_ry)
+    w, s, push = eliminate_coefficients(link_y, gl_y, gr_y, r_y, work_c, work_d)
+    coef_y[my_row, :NZ, :] = w
+    coef_y[my_row, NZ : 2 * NZ, :] = s
+    coef_y[my_row, 2 * NZ :, :] = push
+    gather_cy.start()
     gather_cx.wait()
     factor_chain(n_col, coef_x, chain_gx, chain_rx)
     gather_rx.wait()
@@ -448,6 +463,8 @@
     rhs_y[my_row, :NZ, :] = d
     rhs_y[my_row, NZ:, :] = push
     gather_ry.start()
+    gather_cy.wait()
+    factor_chain(n_row, coef_y, chain_gy, chain_ry)
     gather_ry.wait()
     solve_chain(n_row, rhs_y, chain_gy, chain_ry, chain_vy)
 
@@ -456,11 +473,8 @@
             out[pl.ds(first + i, NZ, stride=L), :] = values[i]
 
     substitute(chain_vy[my_row], chain_vy[my_row + 1], gl_y, gr_y, work_b, work_a, store_y)
-    result = pltpu.make_async_copy(out, out_hbm, out_sem)
-    result.start()
     for transfer in (share_y, share_x, gather_cx, gather_rx, gather_cy, gather_ry):
         transfer.finish()
-    result.wait()
 
 
 def solution(mesh):
@@ -473,6 +487,8 @@
         whole = pltpu.VMEM((NZ * L, L), jnp.float32)
         integer = pltpu.VMEM((NZ * L, L), jnp.int32)
 
+        parameter = pltpu.SMEM((3,), jnp.float32)
+
         def stack(count, height):
             return pltpu.VMEM((count, height * NZ, L), jnp.float32)
 
@@ -481,16 +497,16 @@
 
         result = pl.pallas_call(
             functools.partial(kernel, n_row, n_col),
-            out_shape=jax.ShapeDtypeStruct((NZ * L, L), jnp.float32),
-            in_specs=[pl.BlockSpec(memory_space=pltpu.SMEM)] * 2 + [pl.BlockSpec(memory_space=pl.ANY)] * 3,
-            out_specs=pl.BlockSpec(memory_space=pl.ANY),
-            scratch_shapes=[whole, integer]
+            out_shape=pltpu.VMEM((NZ * L, L), jnp.float32),
+            in_specs=[pl.BlockSpec(memory_space=pltpu.HBM)] * 5,
+            out_specs=pl.BlockSpec(memory_space=pltpu.VMEM),
+            scratch_shapes=[parameter, parameter, whole, integer]
             + [whole] * 19
             + [stack(2, 2)] * 4
             + [stack(n_col, 3), stack(n_col, 2), stack(n_row, 3), stack(n_row, 2)]
             + [stack(n_col, 1), stack(n_col, 1), stack(n_col + 1, 1)]
             + [stack(n_row, 1), stack(n_row, 1), stack(n_row + 1, 1)]
-            + [dma(3), pltpu.SemaphoreType.DMA]
+            + [dma(2), pltpu.SemaphoreType.DMA((3, NZ))]
             + [dma(2)] * 4
             + [dma(n_col - 1)] * 4
             + [dma(n_row - 1)] * 4,
@@ -500,7 +516,7 @@
             cost_estimate=pl.CostEstimate(
                 flops=20_000_000, bytes_accessed=2_200_000, transcendentals=400_000
             ),
-        )(mag, rate, flat(field), flat(region), flat(source))
+        )(*[pltpu.with_memory_space_constraint(v, pltpu.HBM) for v in (mag, rate, flat(field), flat(region), flat(source))])
         return result.reshape(NZ, L, L)
 
     spec = P(None, "row", "col")

time: 24.2 us -> 19.7 us (0.81)
  local copies, waits for them, and re-layouts: 4.59 us -> 0.8 us
  Pallas kernels: 19.3 us -> 18.7 us
    unnamed x11 -> x1, local copies, waits for them, and re-layouts: 4.59 us -> 0.8 us
    pallas_call x1, Pallas kernels: 19.3 us -> 18.7 us  [local(): pl.pallas_call(functools.partial(kernel, n_row, n_col), out_shape=pltpu.V...]
where the time goes in v2:
time: 19.7 us; the launch traced here: 19.6 us
  Pallas kernels  18.7 us (95%)
  local copies, waits for them, and re-layouts  0.8 us (4%)
    pallas_call x1, Pallas kernels, local(): pl.pallas_call(functools.partial(kernel, n_row, n_col), out_shape=pltpu.V...  18.7 us
    unnamed x1, local copies, waits for them, and re-layouts  0.8 us

profile of v2, /device:TPU:0, one launch (start us, length us, event | category | flops | bytes accessed | tf_op | source)
XLA Modules:
  0.0 19.6 jit_solution(14421789839063357300)
XLA Ops:
  0.0 18.7 %shard_map.55 = f32[1024,128]{1,0:T(8,128)S(1)} custom-call(f32[3]{0:T(128)} %mag_hbm.1, f32[3]{0:T(128)} %rate_hbm.1, f32[1024,128]{1,0:T(8,128)} %bitcast.5, s32[1024,128]{1,0:T(8,128)} %bitcast.6, f32[1024,128]{1,0:T(8,128)} %bitcast.7), custom_call_target="tpu_custom_call" | custom-call | flops 20000000 | bytes 2200000 | tf_op jit(solution)/shard_map/pallas_call | solution.py:498
  18.8 0.8 %copy.7 = f32[8,128,128]{2,1,0:T(8,128)} copy(f32[8,128,128]{2,1,0:T(8,128)S(1)} %bitcast.4) | data formatting | bytes 1048576

commit v3 on v2

--- a/solution.py
+++ b/solution.py
@@ -84,14 +84,14 @@
     return w_ref[pl.ds((L - 2) * NZ, NZ), :], s_ref[pl.ds((L - 2) * NZ, NZ), :], pushed_out[0]
 
 
-def eliminate_right_side(side_ref, gl_ref, gr_ref, r_ref, d_ref, q_ref):
+def eliminate_right_side(load_side, gl_ref, gr_ref, r_ref, d_ref, q_ref):
     pushed_out = jnp.zeros((1, NZ, L), jnp.float32)
     for count, half, node_at, pair_at in levels():
         block = min(half, BLOCK)
         carry = jnp.zeros((1, NZ, L), jnp.float32)
         for first in reversed(range(0, half, block)):
             if count == L:
-                de, do = pairs(nodes(side_ref, 2 * first, 2 * block))
+                de, do = pairs(load_side(2 * first, 2 * block))
             else:
                 de, do = pairs(nodes(d_ref, node_at + 2 * first, 2 * block))
             push = nodes(gl_ref, pair_at + first, block) * de
@@ -268,6 +268,7 @@
     field_x,
     cond_x,
     side_x,
+    extra_x,
     link_x,
     solved,
     gl_x,
@@ -309,26 +310,6 @@
     ry_send,
     ry_recv,
 ):
-    parameters = [
-        pltpu.make_async_copy(mag_hbm, mag, par_sem.at[0]),
-        pltpu.make_async_copy(rate_hbm, rate, par_sem.at[1]),
-    ]
-    for load in parameters:
-        load.start()
-
-    def layer(source_ref, target_ref, kind, z):
-        rows = pl.ds(z * L, L)
-        return pltpu.make_async_copy(source_ref.at[rows], target_ref.at[rows], in_sem.at[kind, z])
-
-    loads = [
-        (layer(field_hbm, field, 0, z), layer(region_hbm, region, 1, z)) for z in range(NZ)
-    ]
-    source_loads = [layer(source_hbm, source, 2, z) for z in range(NZ)]
-    for field_load, region_load in loads:
-        field_load.start()
-        region_load.start()
-    for load in source_loads:
-        load.start()
     my_row, my_col = lax.axis_index("row"), lax.axis_index("col")
     barrier = pltpu.get_barrier_semaphore()
     for step in range(1, n_row):
@@ -340,6 +321,26 @@
             barrier, inc=1, device_id={"col": lax.rem(my_col + step, n_col)}, device_id_type=MESH
         )
 
+    parameters = [
+        pltpu.make_async_copy(mag_hbm, mag, par_sem.at[0]),
+        pltpu.make_async_copy(rate_hbm, rate, par_sem.at[1]),
+    ]
+    for load in parameters:
+        load.start()
+
+    def layers(source_ref, target_ref, kind, z, count=2):
+        rows = pl.ds(z * L, count * L)
+        return pltpu.make_async_copy(source_ref.at[rows], target_ref.at[rows], in_sem.at[kind, z])
+
+    loads = [
+        (layers(field_hbm, field, 0, z), layers(region_hbm, region, 1, z)) for z in range(0, NZ, 2)
+    ]
+    source_load = layers(source_hbm, source, 2, 0, NZ)
+    for field_load, region_load in loads:
+        field_load.start()
+        region_load.start()
+    source_load.start()
+
     share_y = Halo("row", n_row, edges_y, halo_y, hy_send, hy_recv)
     share_x = Halo("col", n_col, edges_x, halo_x, hx_send, hx_recv)
     gather_cx = Gather("col", n_col, coef_x, cx_send, cx_recv)
@@ -360,8 +361,9 @@
 
     for z in range(NZ):
         rows = pl.ds(z * L, L)
-        for load in loads[z]:
-            load.wait()
+        if z % 2 == 0:
+            for load in loads[z // 2]:
+                load.wait()
         cond[rows, :] = conductivity(field[rows, :], region[rows, :])
     for side, y in ((0, 0), (1, L - 1)):
         edges_y[side, :NZ, :] = field[pl.ds(y, NZ, stride=L), :]
@@ -395,8 +397,29 @@
             half_y[pl.ds((first - 1) * NZ, NZ), :] = flux[0] - flux_before
         t_before, c_before, flux_before = t[-1:], c[-1:], flux[-1]
 
-    for load in source_loads:
-        load.wait()
+    share_x.wait()
+    t_before, c_before = halo_x[0, :NZ, :][None], halo_x[0, NZ:, :][None]
+    flux_before = None
+    for first in range(0, L + 1, BLOCK):
+        if first < L:
+            t, c = nodes(field_x, first, BLOCK), nodes(cond_x, first, BLOCK)
+        else:
+            t, c = halo_x[1, :NZ, :][None], halo_x[1, NZ:, :][None]
+        weight, flux = links(c, t, c_before, t_before)
+        if first < L:
+            put_nodes(link_x, first, weight)
+            extra = shifted_up(flux, jnp.zeros((1, NZ, L), jnp.float32)) - flux
+            put_nodes(extra_x, first, extra)
+        if first > 0:
+            at = pl.ds((first - 1) * NZ, NZ)
+            extra_x[at, :] = extra_x[at, :] + flux[0]
+        t_before, c_before = t[-1:], c[-1:]
+    w, s, push = eliminate_coefficients(link_x, gl_x, gr_x, r_x, work_a, work_b)
+    coef_x[my_col, :NZ, :] = w
+    coef_x[my_col, NZ : 2 * NZ, :] = s
+    coef_x[my_col, 2 * NZ :, :] = push
+    gather_cx.start()
+    source_load.wait()
     lower = None
     for z in range(NZ):
         rows = pl.ds(z * L, L)
@@ -414,29 +437,10 @@
         total = t + 2.0 * half_y[pl.ds(z, L, stride=NZ), :] + along_z + source[rows, :]
         side_x[pl.ds(z, L, stride=NZ), :] = total.T
 
-    share_x.wait()
-    t_before, c_before = halo_x[0, :NZ, :][None], halo_x[0, NZ:, :][None]
-    flux_before = None
-    for first in range(0, L + 1, BLOCK):
-        if first < L:
-            t, c = nodes(field_x, first, BLOCK), nodes(cond_x, first, BLOCK)
-        else:
-            t, c = halo_x[1, :NZ, :][None], halo_x[1, NZ:, :][None]
-        weight, flux = links(c, t, c_before, t_before)
-        if first < L:
-            put_nodes(link_x, first, weight)
-            extra = shifted_up(flux, jnp.zeros((1, NZ, L), jnp.float32)) - flux
-            put_nodes(side_x, first, nodes(side_x, first, BLOCK) + extra)
-        if first > 0:
-            at = pl.ds((first - 1) * NZ, NZ)
-            side_x[at, :] = side_x[at, :] + flux[0]
-        t_before, c_before = t[-1:], c[-1:]
-    w, s, push = eliminate_coefficients(link_x, gl_x, gr_x, r_x, work_a, work_b)
-    coef_x[my_col, :NZ, :] = w
-    coef_x[my_col, NZ : 2 * NZ, :] = s
-    coef_x[my_col, 2 * NZ :, :] = push
-    gather_cx.start()
-    d, push = eliminate_right_side(side_x, gl_x, gr_x, r_x, work_a, work_b)
+    def side_of_x(first, count):
+        return nodes(side_x, first, count) + nodes(extra_x, first, count)
+
+    d, push = eliminate_right_side(side_of_x, gl_x, gr_x, r_x, work_a, work_b)
     rhs_x[my_col, :NZ, :] = d
     rhs_x[my_col, NZ:, :] = push
     gather_rx.start()
@@ -459,7 +463,10 @@
     for z in range(NZ):
         at = pl.ds(z, L, stride=NZ)
         side_x[at, :] = solved[at, :].T - half_y[at, :]
-    d, push = eliminate_right_side(side_x, gl_y, gr_y, r_y, work_a, work_b)
+    def side_of_y(first, count):
+        return nodes(side_x, first, count)
+
+    d, push = eliminate_right_side(side_of_y, gl_y, gr_y, r_y, work_a, work_b)
     rhs_y[my_row, :NZ, :] = d
     rhs_y[my_row, NZ:, :] = push
     gather_ry.start()
@@ -501,7 +508,7 @@
             in_specs=[pl.BlockSpec(memory_space=pltpu.HBM)] * 5,
             out_specs=pl.BlockSpec(memory_space=pltpu.VMEM),
             scratch_shapes=[parameter, parameter, whole, integer]
-            + [whole] * 19
+            + [whole] * 20
             + [stack(2, 2)] * 4
             + [stack(n_col, 3), stack(n_col, 2), stack(n_row, 3), stack(n_row, 2)]
             + [stack(n_col, 1), stack(n_col, 1), stack(n_col + 1, 1)]

time: 19.7 us -> 19.4 us (0.985)
  Pallas kernels: 18.7 us -> 18.5 us
    pallas_call x1, Pallas kernels: 18.7 us -> 18.5 us  [local(): pl.pallas_call(functools.partial(kernel, n_row, n_col), out_shape=pltpu.V...]
where the time goes in v3:
time: 19.4 us; the launch traced here: 19.3 us
  Pallas kernels  18.5 us (95%)
  local copies, waits for them, and re-layouts  0.8 us (4%)
    pallas_call x1, Pallas kernels, local(): pl.pallas_call(functools.partial(kernel, n_row, n_col), out_shape=pltpu.V...  18.5 us
    unnamed x1, local copies, waits for them, and re-layouts  0.8 us

profile of v3, /device:TPU:0, one launch (start us, length us, event | category | flops | bytes accessed | tf_op | source)
XLA Modules:
  0.0 19.3 jit_solution(14336901627158403147)
XLA Ops:
  0.0 18.5 %shard_map.55 = f32[1024,128]{1,0:T(8,128)S(1)} custom-call(f32[3]{0:T(128)} %mag_hbm.1, f32[3]{0:T(128)} %rate_hbm.1, f32[1024,128]{1,0:T(8,128)} %bitcast.5, s32[1024,128]{1,0:T(8,128)} %bitcast.6, f32[1024,128]{1,0:T(8,128)} %bitcast.7), custom_call_target="tpu_custom_call" | custom-call | flops 20000000 | bytes 2200000 | tf_op jit(solution)/shard_map/pallas_call | solution.py:505
  18.5 0.8 %copy.7 = f32[8,128,128]{2,1,0:T(8,128)} copy(f32[8,128,128]{2,1,0:T(8,128)S(1)} %bitcast.4) | data formatting | bytes 1048576

commit v4 on v3

--- a/solution.py
+++ b/solution.py
@@ -13,6 +13,7 @@
 
 NZ = 8
 L = 128
+PITCH = L + 8
 BLOCK = 16
 
 
@@ -263,6 +264,7 @@
     region,
     source,
     cond,
+    wide,
     half_y,
     link_y,
     field_x,
@@ -328,18 +330,20 @@
     for load in parameters:
         load.start()
 
-    def layers(source_ref, target_ref, kind, z, count=2):
-        rows = pl.ds(z * L, count * L)
-        return pltpu.make_async_copy(source_ref.at[rows], target_ref.at[rows], in_sem.at[kind, z])
+    def layer(source_ref, target_ref, kind, z):
+        return pltpu.make_async_copy(
+            source_ref.at[pl.ds(z * L, L)], target_ref.at[pl.ds(z * PITCH, L)], in_sem.at[kind, z]
+        )
 
     loads = [
-        (layers(field_hbm, field, 0, z), layers(region_hbm, region, 1, z)) for z in range(0, NZ, 2)
+        (layer(field_hbm, field, 0, z), layer(region_hbm, region, 1, z)) for z in range(NZ)
     ]
-    source_load = layers(source_hbm, source, 2, 0, NZ)
+    source_loads = [layer(source_hbm, source, 2, z) for z in range(NZ)]
     for field_load, region_load in loads:
         field_load.start()
         region_load.start()
-    source_load.start()
+    for load in source_loads:
+        load.start()
 
     share_y = Halo("row", n_row, edges_y, halo_y, hy_send, hy_recv)
     share_x = Halo("col", n_col, edges_x, halo_x, hx_send, hx_recv)
@@ -360,19 +364,18 @@
         return scale * jnp.exp(-soft * kelvin)
 
     for z in range(NZ):
-        rows = pl.ds(z * L, L)
-        if z % 2 == 0:
-            for load in loads[z // 2]:
-                load.wait()
+        rows = pl.ds(z * PITCH, L)
+        for load in loads[z]:
+            load.wait()
         cond[rows, :] = conductivity(field[rows, :], region[rows, :])
     for side, y in ((0, 0), (1, L - 1)):
-        edges_y[side, :NZ, :] = field[pl.ds(y, NZ, stride=L), :]
-        edges_y[side, NZ:, :] = cond[pl.ds(y, NZ, stride=L), :]
+        edges_y[side, :NZ, :] = field[pl.ds(y, NZ, stride=PITCH), :]
+        edges_y[side, NZ:, :] = cond[pl.ds(y, NZ, stride=PITCH), :]
     pl.semaphore_wait(barrier, n_row + n_col - 2)
     share_y.start()
 
     for z in range(NZ):
-        rows = pl.ds(z * L, L)
+        rows = pl.ds(z * PITCH, L)
         field_x[pl.ds(z, L, stride=NZ), :] = field[rows, :].T
         cond_x[pl.ds(z, L, stride=NZ), :] = cond[rows, :].T
     for side, x in ((0, 0), (1, L - 1)):
@@ -385,8 +388,8 @@
     flux_before = None
     for first in range(0, L + 1, BLOCK):
         if first < L:
-            t = jnp.stack([field[pl.ds(first + i, NZ, stride=L), :] for i in range(BLOCK)])
-            c = jnp.stack([cond[pl.ds(first + i, NZ, stride=L), :] for i in range(BLOCK)])
+            t = jnp.stack([field[pl.ds(first + i, NZ, stride=PITCH), :] for i in range(BLOCK)])
+            c = jnp.stack([cond[pl.ds(first + i, NZ, stride=PITCH), :] for i in range(BLOCK)])
         else:
             t, c = halo_y[1, :NZ, :][None], halo_y[1, NZ:, :][None]
         weight, flux = links(c, t, c_before, t_before)
@@ -419,15 +422,16 @@
     coef_x[my_col, NZ : 2 * NZ, :] = s
     coef_x[my_col, 2 * NZ :, :] = push
     gather_cx.start()
-    source_load.wait()
+    for load in source_loads:
+        load.wait()
     lower = None
     for z in range(NZ):
-        rows = pl.ds(z * L, L)
+        rows = pl.ds(z * PITCH, L)
         t, c = field[rows, :], cond[rows, :]
         if z == 0:
             lower = depth_ratio * c * t
         if z < NZ - 1:
-            above = pl.ds((z + 1) * L, L)
+            above = pl.ds((z + 1) * PITCH, L)
             ta, ca = field[above, :], cond[above, :]
             upper = (2.0 * depth_ratio) * c * ca * inverse(c + ca) * (ta - t)
             along_z = upper - lower
@@ -477,9 +481,11 @@
 
     def store_y(first, values):
         for i in range(values.shape[0]):
-            out[pl.ds(first + i, NZ, stride=L), :] = values[i]
+            wide[pl.ds(first + i, NZ, stride=PITCH), :] = values[i]
 
     substitute(chain_vy[my_row], chain_vy[my_row + 1], gl_y, gr_y, work_b, work_a, store_y)
+    for z in range(NZ):
+        out[pl.ds(z * L, L), :] = wide[pl.ds(z * PITCH, L), :]
     for transfer in (share_y, share_x, gather_cx, gather_rx, gather_cy, gather_ry):
         transfer.finish()
 
@@ -492,7 +498,8 @@
             return values.reshape(NZ * L, L)
 
         whole = pltpu.VMEM((NZ * L, L), jnp.float32)
-        integer = pltpu.VMEM((NZ * L, L), jnp.int32)
+        pitched = pltpu.VMEM((NZ * PITCH, L), jnp.float32)
+        integer = pltpu.VMEM((NZ * PITCH, L), jnp.int32)
 
         parameter = pltpu.SMEM((3,), jnp.float32)
 
@@ -507,8 +514,9 @@
             out_shape=pltpu.VMEM((NZ * L, L), jnp.float32),
             in_specs=[pl.BlockSpec(memory_space=pltpu.HBM)] * 5,
             out_specs=pl.BlockSpec(memory_space=pltpu.VMEM),
-            scratch_shapes=[parameter, parameter, whole, integer]
-            + [whole] * 20
+            scratch_shapes=[parameter, parameter, pitched, integer]
+            + [pitched] * 3
+            + [whole] * 18
             + [stack(2, 2)] * 4
             + [stack(n_col, 3), stack(n_col, 2), stack(n_row, 3), stack(n_row, 2)]
             + [stack(n_col, 1), stack(n_col, 1), stack(n_col + 1, 1)]

time: 19.4 us -> 19 us (0.979)
  Pallas kernels: 18.5 us -> 18.1 us
    pallas_call x1, Pallas kernels: 18.5 us -> 18.1 us  [local(): pl.pallas_call(functools.partial(kernel, n_row, n_col), out_shape=pltpu.V...]
where the time goes in v4:
time: 19 us; the launch traced here: 18.9 us
  Pallas kernels  18.1 us (95%)
  local copies, waits for them, and re-layouts  0.8 us (4%)
    pallas_call x1, Pallas kernels, local(): pl.pallas_call(functools.partial(kernel, n_row, n_col), out_shape=pltpu.V...  18.1 us
    unnamed x1, local copies, waits for them, and re-layouts  0.8 us

profile of v4, /device:TPU:0, one launch (start us, length us, event | category | flops | bytes accessed | tf_op | source)
XLA Modules:
  0.0 18.9 jit_solution(11734439528548012529)
XLA Ops:
  0.0 18.1 %shard_map.55 = f32[1024,128]{1,0:T(8,128)S(1)} custom-call(f32[3]{0:T(128)} %mag_hbm.1, f32[3]{0:T(128)} %rate_hbm.1, f32[1024,128]{1,0:T(8,128)} %bitcast.5, s32[1024,128]{1,0:T(8,128)} %bitcast.6, f32[1024,128]{1,0:T(8,128)} %bitcast.7), custom_call_target="tpu_custom_call" | custom-call | flops 20000000 | bytes 2200000 | tf_op jit(solution)/shard_map/pallas_call | solution.py:512
  18.1 0.8 %copy.7 = f32[8,128,128]{2,1,0:T(8,128)} copy(f32[8,128,128]{2,1,0:T(8,128)S(1)} %bitcast.4) | data formatting | bytes 1048576

commit v5 on v4

--- a/solution.py
+++ b/solution.py
@@ -243,10 +243,39 @@
             self.copy(1).wait_send()
 
 
-def links(cond, field, cond_before, field_before):
-    beside = shifted_down(cond, cond_before)
-    weight = (2.0 * inplane_half) * cond * beside * inverse(cond + beside)
-    return weight, weight * (field - shifted_down(field, field_before))
+def link_between(cond, field, cond_before, field_before):
+    weight = (2.0 * inplane_half) * cond * cond_before * inverse(cond + cond_before)
+    return weight, weight * (field - field_before)
+
+
+def inner_links(field_rows, cond_rows, link_ref, sum_ref):
+    flux_before = None
+    for first in range(0, L, BLOCK):
+        t, c = field_rows(first), cond_rows(first)
+        if first == 0:
+            t_before, c_before = t[:1], c[:1]
+        weight, flux = link_between(
+            c, t, shifted_down(c, c_before), shifted_down(t, t_before)
+        )
+        put_nodes(link_ref, first, weight)
+        put_nodes(sum_ref, first, shifted_up(flux, jnp.zeros((1, NZ, L), jnp.float32)) - flux)
+        if first > 0:
+            at = pl.ds((first - 1) * NZ, NZ)
+            sum_ref[at, :] = flux[0] - flux_before
+        t_before, c_before, flux_before = t[-1:], c[-1:], flux[-1]
+
+
+def edge_links(edges, halo, link_ref, sum_ref):
+    weight, flux = link_between(
+        edges[0, NZ:, :], edges[0, :NZ, :], halo[0, NZ:, :], halo[0, :NZ, :]
+    )
+    link_ref[pl.ds(0, NZ), :] = weight
+    sum_ref[pl.ds(0, NZ), :] = sum_ref[pl.ds(0, NZ), :] - flux
+    weight, flux = link_between(
+        halo[1, NZ:, :], halo[1, :NZ, :], edges[1, NZ:, :], edges[1, :NZ, :]
+    )
+    at = pl.ds((L - 1) * NZ, NZ)
+    sum_ref[at, :] = sum_ref[at, :] + flux
 
 
 def kernel(
@@ -367,61 +396,30 @@
         rows = pl.ds(z * PITCH, L)
         for load in loads[z]:
             load.wait()
-        cond[rows, :] = conductivity(field[rows, :], region[rows, :])
-    for side, y in ((0, 0), (1, L - 1)):
-        edges_y[side, :NZ, :] = field[pl.ds(y, NZ, stride=PITCH), :]
-        edges_y[side, NZ:, :] = cond[pl.ds(y, NZ, stride=PITCH), :]
+        kelvin = field[rows, :]
+        value = conductivity(kelvin, region[rows, :])
+        cond[rows, :] = value
+        field_x[pl.ds(z, L, stride=NZ), :] = kelvin.T
+        cond_x[pl.ds(z, L, stride=NZ), :] = value.T
+    for side, at in ((0, 0), (1, L - 1)):
+        edges_y[side, :NZ, :] = field[pl.ds(at, NZ, stride=PITCH), :]
+        edges_y[side, NZ:, :] = cond[pl.ds(at, NZ, stride=PITCH), :]
+        edges_x[side, :NZ, :] = field_x[pl.ds(at * NZ, NZ), :]
+        edges_x[side, NZ:, :] = cond_x[pl.ds(at * NZ, NZ), :]
     pl.semaphore_wait(barrier, n_row + n_col - 2)
+    share_x.start()
     share_y.start()
 
-    for z in range(NZ):
-        rows = pl.ds(z * PITCH, L)
-        field_x[pl.ds(z, L, stride=NZ), :] = field[rows, :].T
-        cond_x[pl.ds(z, L, stride=NZ), :] = cond[rows, :].T
-    for side, x in ((0, 0), (1, L - 1)):
-        edges_x[side, :NZ, :] = field_x[pl.ds(x * NZ, NZ), :]
-        edges_x[side, NZ:, :] = cond_x[pl.ds(x * NZ, NZ), :]
-    share_x.start()
-
-    share_y.wait()
-    t_before, c_before = halo_y[0, :NZ, :][None], halo_y[0, NZ:, :][None]
-    flux_before = None
-    for first in range(0, L + 1, BLOCK):
-        if first < L:
-            t = jnp.stack([field[pl.ds(first + i, NZ, stride=PITCH), :] for i in range(BLOCK)])
-            c = jnp.stack([cond[pl.ds(first + i, NZ, stride=PITCH), :] for i in range(BLOCK)])
-        else:
-            t, c = halo_y[1, :NZ, :][None], halo_y[1, NZ:, :][None]
-        weight, flux = links(c, t, c_before, t_before)
-        if first < L:
-            put_nodes(link_y, first, weight)
-            put_nodes(half_y, first, shifted_up(flux, flux[-1:]) - flux)
-        if flux_before is not None:
-            half_y[pl.ds((first - 1) * NZ, NZ), :] = flux[0] - flux_before
-        t_before, c_before, flux_before = t[-1:], c[-1:], flux[-1]
-
-    share_x.wait()
-    t_before, c_before = halo_x[0, :NZ, :][None], halo_x[0, NZ:, :][None]
-    flux_before = None
-    for first in range(0, L + 1, BLOCK):
-        if first < L:
-            t, c = nodes(field_x, first, BLOCK), nodes(cond_x, first, BLOCK)
-        else:
-            t, c = halo_x[1, :NZ, :][None], halo_x[1, NZ:, :][None]
-        weight, flux = links(c, t, c_before, t_before)
-        if first < L:
-            put_nodes(link_x, first, weight)
-            extra = shifted_up(flux, jnp.zeros((1, NZ, L), jnp.float32)) - flux
-            put_nodes(extra_x, first, extra)
-        if first > 0:
-            at = pl.ds((first - 1) * NZ, NZ)
-            extra_x[at, :] = extra_x[at, :] + flux[0]
-        t_before, c_before = t[-1:], c[-1:]
-    w, s, push = eliminate_coefficients(link_x, gl_x, gr_x, r_x, work_a, work_b)
-    coef_x[my_col, :NZ, :] = w
-    coef_x[my_col, NZ : 2 * NZ, :] = s
-    coef_x[my_col, 2 * NZ :, :] = push
-    gather_cx.start()
+    def y_rows(ref, first):
+        return jnp.stack([ref[pl.ds(first + i, NZ, stride=PITCH), :] for i in range(BLOCK)])
+
+    def x_rows(ref, first):
+        return nodes(ref, first, BLOCK)
+
+    inner_links(functools.partial(y_rows, field), functools.partial(y_rows, cond), link_y, half_y)
+    inner_links(
+        functools.partial(x_rows, field_x), functools.partial(x_rows, cond_x), link_x, extra_x
+    )
     for load in source_loads:
         load.wait()
     lower = None
@@ -438,7 +436,20 @@
             lower = upper
         else:
             along_z = -lower
-        total = t + 2.0 * half_y[pl.ds(z, L, stride=NZ), :] + along_z + source[rows, :]
+        source[rows, :] = t + along_z + source[rows, :]
+
+    share_x.wait()
+    edge_links(edges_x, halo_x, link_x, extra_x)
+    w, s, push = eliminate_coefficients(link_x, gl_x, gr_x, r_x, work_a, work_b)
+    coef_x[my_col, :NZ, :] = w
+    coef_x[my_col, NZ : 2 * NZ, :] = s
+    coef_x[my_col, 2 * NZ :, :] = push
+    gather_cx.start()
+
+    share_y.wait()
+    edge_links(edges_y, halo_y, link_y, half_y)
+    for z in range(NZ):
+        total = source[pl.ds(z * PITCH, L), :] + 2.0 * half_y[pl.ds(z, L, stride=NZ), :]
         side_x[pl.ds(z, L, stride=NZ), :] = total.T
 
     def side_of_x(first, count):

time: 19 us -> 18.8 us (0.989)
  Pallas kernels: 18.1 us -> 17.9 us
    pallas_call x1, Pallas kernels: 18.1 us -> 17.9 us  [local(): pl.pallas_call(functools.partial(kernel, n_row, n_col), out_shape=pltpu.V...]
where the time goes in v5:
time: 18.8 us; the launch traced here: 18.7 us
  Pallas kernels  17.9 us (95%)
  local copies, waits for them, and re-layouts  0.8 us (4%)
    pallas_call x1, Pallas kernels, local(): pl.pallas_call(functools.partial(kernel, n_row, n_col), out_shape=pltpu.V...  17.9 us
    unnamed x1, local copies, waits for them, and re-layouts  0.8 us

profile of v5, /device:TPU:0, one launch (start us, length us, event | category | flops | bytes accessed | tf_op | source)
XLA Modules:
  0.0 18.7 jit_solution(14903890838356873772)
XLA Ops:
  0.0 17.9 %shard_map.55 = f32[1024,128]{1,0:T(8,128)S(1)} custom-call(f32[3]{0:T(128)} %mag_hbm.1, f32[3]{0:T(128)} %rate_hbm.1, f32[1024,128]{1,0:T(8,128)} %bitcast.5, s32[1024,128]{1,0:T(8,128)} %bitcast.6, f32[1024,128]{1,0:T(8,128)} %bitcast.7), custom_call_target="tpu_custom_call" | custom-call | flops 20000000 | bytes 2200000 | tf_op jit(solution)/shard_map/pallas_call | solution.py:523
  17.9 0.8 %copy.7 = f32[8,128,128]{2,1,0:T(8,128)} copy(f32[8,128,128]{2,1,0:T(8,128)S(1)} %bitcast.4) | data formatting | bytes 1048576

commit v6 on v5

--- a/solution.py
+++ b/solution.py
@@ -383,6 +383,9 @@
 
     for load in parameters:
         load.wait()
+    for field_load, region_load in loads:
+        field_load.wait()
+        region_load.wait()
     m0, m1, m2 = mag[0], mag[1], mag[2]
     k0, k1, k2 = rate[0], rate[1], rate[2]
 
@@ -394,8 +397,6 @@
 
     for z in range(NZ):
         rows = pl.ds(z * PITCH, L)
-        for load in loads[z]:
-            load.wait()
         kelvin = field[rows, :]
         value = conductivity(kelvin, region[rows, :])
         cond[rows, :] = value

time: 18.8 us -> 18.7 us (level)
  Pallas kernels: 17.9 us -> 17.7 us
where the time goes in v6:
time: 18.7 us; the launch traced here: 18.5 us
  Pallas kernels  17.7 us (95%)
  local copies, waits for them, and re-layouts  0.8 us (4%)
    pallas_call x1, Pallas kernels, local(): pl.pallas_call(functools.partial(kernel, n_row, n_col), out_shape=pltpu.V...  17.7 us
    unnamed x1, local copies, waits for them, and re-layouts  0.8 us

profile of v6, /device:TPU:0, one launch (start us, length us, event | category | flops | bytes accessed | tf_op | source)
XLA Modules:
  0.0 18.5 jit_solution(18213797115563409843)
XLA Ops:
  0.0 17.7 %shard_map.55 = f32[1024,128]{1,0:T(8,128)S(1)} custom-call(f32[3]{0:T(128)} %mag_hbm.1, f32[3]{0:T(128)} %rate_hbm.1, f32[1024,128]{1,0:T(8,128)} %bitcast.5, s32[1024,128]{1,0:T(8,128)} %bitcast.6, f32[1024,128]{1,0:T(8,128)} %bitcast.7), custom_call_target="tpu_custom_call" | custom-call | flops 20000000 | bytes 2200000 | tf_op jit(solution)/shard_map/pallas_call | solution.py:524
  17.7 0.8 %copy.7 = f32[8,128,128]{2,1,0:T(8,128)} copy(f32[8,128,128]{2,1,0:T(8,128)S(1)} %bitcast.4) | data formatting | bytes 1048576

commit v7 on v6

--- a/solution.py
+++ b/solution.py
@@ -189,6 +189,52 @@
     def finish(self):
         for step in range(1, self.n):
             self.copy(step, self.me).wait_send()
+
+
+class PairedGather:
+    def __init__(self, axis, n, buffer, send, recv):
+        self.axis, self.n, self.buffer, self.send, self.recv = axis, n, buffer, send, recv
+        self.me = lax.axis_index(axis)
+        self.beside = self.me + 1 - 2 * lax.rem(self.me, 2)
+
+    def copy(self, slot, to, at):
+        return pltpu.make_async_remote_copy(
+            src_ref=self.buffer.at[slot],
+            dst_ref=self.buffer.at[slot],
+            send_sem=self.send.at[at],
+            recv_sem=self.recv.at[at],
+            device_id={self.axis: to},
+            device_id_type=MESH,
+        )
+
+    def out(self, step):
+        return self.copy(self.me, lax.rem(self.me + step, self.n), step - 1)
+
+    def relayed(self, step):
+        return self.copy(lax.rem(self.me + self.n - step, self.n), self.beside, step)
+
+    def start(self):
+        for step in range(2, self.n, 2):
+            self.out(step).start()
+        self.copy(self.me, self.beside, 0).start()
+
+    def relay(self):
+        for step in range(2, self.n, 2):
+            slot = lax.rem(self.me + self.n - step, self.n)
+            self.copy(slot, self.beside, step - 1).wait_recv()
+            self.relayed(step).start()
+
+    def wait(self):
+        self.copy(self.beside, self.beside, 0).wait_recv()
+        for step in range(2, self.n, 2):
+            slot = lax.rem(self.beside + self.n - step, self.n)
+            self.copy(slot, self.beside, step).wait_recv()
+
+    def finish(self):
+        self.copy(self.me, self.beside, 0).wait_send()
+        for step in range(2, self.n, 2):
+            self.out(step).wait_send()
+            self.relayed(step).wait_send()
 
 
 class Halo:
@@ -376,8 +422,8 @@
 
     share_y = Halo("row", n_row, edges_y, halo_y, hy_send, hy_recv)
     share_x = Halo("col", n_col, edges_x, halo_x, hx_send, hx_recv)
-    gather_cx = Gather("col", n_col, coef_x, cx_send, cx_recv)
-    gather_rx = Gather("col", n_col, rhs_x, rx_send, rx_recv)
+    gather_cx = PairedGather("col", n_col, coef_x, cx_send, cx_recv)
+    gather_rx = PairedGather("col", n_col, rhs_x, rx_send, rx_recv)
     gather_cy = Gather("row", n_row, coef_y, cy_send, cy_recv)
     gather_ry = Gather("row", n_row, rhs_y, ry_send, ry_recv)
 
@@ -466,8 +512,10 @@
     coef_y[my_row, NZ : 2 * NZ, :] = s
     coef_y[my_row, 2 * NZ :, :] = push
     gather_cy.start()
+    gather_cx.relay()
     gather_cx.wait()
     factor_chain(n_col, coef_x, chain_gx, chain_rx)
+    gather_rx.relay()
     gather_rx.wait()
     solve_chain(n_col, rhs_x, chain_gx, chain_rx, chain_vx)
 

time: 18.7 us -> 18.9 us (1.011)
  Pallas kernels: 17.7 us -> 17.9 us
    pallas_call x1, Pallas kernels: 17.7 us -> 17.9 us  [local(): pl.pallas_call(functools.partial(kernel, n_row, n_col), out_shape=pltpu.V...]
where the time goes in v7:
time: 18.9 us; the launch traced here: 18.7 us
  Pallas kernels  17.9 us (95%)
  local copies, waits for them, and re-layouts  0.8 us (4%)
    pallas_call x1, Pallas kernels, local(): pl.pallas_call(functools.partial(kernel, n_row, n_col), out_shape=pltpu.V...  17.9 us
    unnamed x1, local copies, waits for them, and re-layouts  0.8 us

profile of v7, /device:TPU:0, one launch (start us, length us, event | category | flops | bytes accessed | tf_op | source)
XLA Modules:
  0.0 18.7 jit_solution(12460333622636653776)
XLA Ops:
  0.0 17.9 %shard_map.55 = f32[1024,128]{1,0:T(8,128)S(1)} custom-call(f32[3]{0:T(128)} %mag_hbm.1, f32[3]{0:T(128)} %rate_hbm.1, f32[1024,128]{1,0:T(8,128)} %bitcast.5, s32[1024,128]{1,0:T(8,128)} %bitcast.6, f32[1024,128]{1,0:T(8,128)} %bitcast.7), custom_call_target="tpu_custom_call" | custom-call | flops 20000000 | bytes 2200000 | tf_op jit(solution)/shard_map/pallas_call | solution.py:572
  17.9 0.8 %copy.7 = f32[8,128,128]{2,1,0:T(8,128)} copy(f32[8,128,128]{2,1,0:T(8,128)S(1)} %bitcast.4) | data formatting | bytes 1048576

commit v8 on v7

--- a/solution.py
+++ b/solution.py
@@ -423,7 +423,7 @@
     share_y = Halo("row", n_row, edges_y, halo_y, hy_send, hy_recv)
     share_x = Halo("col", n_col, edges_x, halo_x, hx_send, hx_recv)
     gather_cx = PairedGather("col", n_col, coef_x, cx_send, cx_recv)
-    gather_rx = PairedGather("col", n_col, rhs_x, rx_send, rx_recv)
+    gather_rx = Gather("col", n_col, rhs_x, rx_send, rx_recv)
     gather_cy = Gather("row", n_row, coef_y, cy_send, cy_recv)
     gather_ry = Gather("row", n_row, rhs_y, ry_send, ry_recv)
 
@@ -515,7 +515,6 @@
     gather_cx.relay()
     gather_cx.wait()
     factor_chain(n_col, coef_x, chain_gx, chain_rx)
-    gather_rx.relay()
     gather_rx.wait()
     solve_chain(n_col, rhs_x, chain_gx, chain_rx, chain_vx)
 

time: 18.9 us -> 17.7 us (0.937)
  Pallas kernels: 17.9 us -> 16.8 us
    pallas_call x1, Pallas kernels: 17.9 us -> 16.8 us  [local(): pl.pallas_call(functools.partial(kernel, n_row, n_col), out_shape=pltpu.V...]
where the time goes in v8:
time: 17.7 us; the launch traced here: 17.6 us
  Pallas kernels  16.8 us (95%)
  local copies, waits for them, and re-layouts  0.8 us (5%)
    pallas_call x1, Pallas kernels, local(): pl.pallas_call(functools.partial(kernel, n_row, n_col), out_shape=pltpu.V...  16.8 us
    unnamed x1, local copies, waits for them, and re-layouts  0.8 us

profile of v8, /device:TPU:0, one launch (start us, length us, event | category | flops | bytes accessed | tf_op | source)
XLA Modules:
  0.0 17.6 jit_solution(13139978140484972729)
XLA Ops:
  0.0 16.8 %shard_map.55 = f32[1024,128]{1,0:T(8,128)S(1)} custom-call(f32[3]{0:T(128)} %mag_hbm.1, f32[3]{0:T(128)} %rate_hbm.1, f32[1024,128]{1,0:T(8,128)} %bitcast.5, s32[1024,128]{1,0:T(8,128)} %bitcast.6, f32[1024,128]{1,0:T(8,128)} %bitcast.7), custom_call_target="tpu_custom_call" | custom-call | flops 20000000 | bytes 2200000 | tf_op jit(solution)/shard_map/pallas_call | solution.py:571
  16.8 0.8 %copy.7 = f32[8,128,128]{2,1,0:T(8,128)} copy(f32[8,128,128]{2,1,0:T(8,128)S(1)} %bitcast.4) | data formatting | bytes 1048576

commit v9 on v8

--- a/solution.py
+++ b/solution.py
@@ -83,6 +83,32 @@
             put_nodes(s_ref, L - 2 * half + first, surplus)
         pushed_out = pushed_out + carry
     return w_ref[pl.ds((L - 2) * NZ, NZ), :], s_ref[pl.ds((L - 2) * NZ, NZ), :], pushed_out[0]
+
+
+def close_coefficients(link_ref, gl_ref, gr_ref, r_ref, w_ref, s_ref):
+    def one(ref, node):
+        return ref[pl.ds(node * NZ, NZ), :]
+
+    weight, surplus, pushed_out = one(link_ref, 0), 1.0, 0.0
+    for count, half, node_at, pair_at in levels():
+        if count == L:
+            wr, so = one(link_ref, 1), 1.0
+        else:
+            wr, so = one(w_ref, node_at + 1), one(s_ref, node_at + 1)
+        inv = inverse(surplus + weight + wr)
+        gl, gr = weight * inv, wr * inv
+        gl_ref[pl.ds(pair_at * NZ, NZ), :] = gl
+        gr_ref[pl.ds(pair_at * NZ, NZ), :] = gr
+        r_ref[pl.ds(pair_at * NZ, NZ), :] = inv
+        pushed_out = pushed_out + gl * surplus
+        surplus = so + gr * surplus
+        if half > 1:
+            push = one(gl_ref, pair_at + 1)
+            if count < L:
+                push = push * one(s_ref, node_at + 2)
+            surplus = surplus + push
+        weight = gl * wr
+    return weight, surplus, pushed_out
 
 
 def eliminate_right_side(load_side, gl_ref, gr_ref, r_ref, d_ref, q_ref):
@@ -485,9 +511,10 @@
             along_z = -lower
         source[rows, :] = t + along_z + source[rows, :]
 
+    eliminate_coefficients(link_x, gl_x, gr_x, r_x, work_a, work_b)
     share_x.wait()
     edge_links(edges_x, halo_x, link_x, extra_x)
-    w, s, push = eliminate_coefficients(link_x, gl_x, gr_x, r_x, work_a, work_b)
+    w, s, push = close_coefficients(link_x, gl_x, gr_x, r_x, work_a, work_b)
     coef_x[my_col, :NZ, :] = w
     coef_x[my_col, NZ : 2 * NZ, :] = s
     coef_x[my_col, 2 * NZ :, :] = push

time: 17.7 us -> 17.5 us (0.989)
  Pallas kernels: 16.8 us -> 16.5 us
    pallas_call x1, Pallas kernels: 16.8 us -> 16.5 us  [local(): pl.pallas_call(functools.partial(kernel, n_row, n_col), out_shape=pltpu.V...]
where the time goes in v9:
time: 17.5 us; the launch traced here: 17.3 us
  Pallas kernels  16.5 us (94%)
  local copies, waits for them, and re-layouts  0.8 us (5%)
    pallas_call x1, Pallas kernels, local(): pl.pallas_call(functools.partial(kernel, n_row, n_col), out_shape=pltpu.V...  16.5 us
    unnamed x1, local copies, waits for them, and re-layouts  0.8 us

profile of v9, /device:TPU:0, one launch (start us, length us, event | category | flops | bytes accessed | tf_op | source)
XLA Modules:
  0.0 17.3 jit_solution(2820341141418525292)
XLA Ops:
  0.0 16.5 %shard_map.55 = f32[1024,128]{1,0:T(8,128)S(1)} custom-call(f32[3]{0:T(128)} %mag_hbm.1, f32[3]{0:T(128)} %rate_hbm.1, f32[1024,128]{1,0:T(8,128)} %bitcast.5, s32[1024,128]{1,0:T(8,128)} %bitcast.6, f32[1024,128]{1,0:T(8,128)} %bitcast.7), custom_call_target="tpu_custom_call" | custom-call | flops 20000000 | bytes 2200000 | tf_op jit(solution)/shard_map/pallas_call | solution.py:598
  16.5 0.8 %copy.7 = f32[8,128,128]{2,1,0:T(8,128)} copy(f32[8,128,128]{2,1,0:T(8,128)S(1)} %bitcast.4) | data formatting | bytes 1048576

commit v10 on v9

--- a/solution.py
+++ b/solution.py
@@ -189,6 +189,10 @@
         chain_v[p + 1] = value
 
 
+def far_first(n, stride):
+    return sorted(range(stride, n, stride), key=lambda step: (abs(2 * step - n), step))
+
+
 class Gather:
     def __init__(self, axis, n, buffer, send, recv):
         self.axis, self.n, self.buffer, self.send, self.recv = axis, n, buffer, send, recv
@@ -205,7 +209,7 @@
         )
 
     def start(self):
-        for step in range(1, self.n):
+        for step in far_first(self.n, 1):
             self.copy(step, self.me).start()
 
     def wait(self):
@@ -240,7 +244,7 @@
         return self.copy(lax.rem(self.me + self.n - step, self.n), self.beside, step)
 
     def start(self):
-        for step in range(2, self.n, 2):
+        for step in far_first(self.n, 2):
             self.out(step).start()
         self.copy(self.me, self.beside, 0).start()
 

time: 17.5 us -> 17.7 us (1.011)
  Pallas kernels: 16.5 us -> 16.7 us
    pallas_call x1, Pallas kernels: 16.5 us -> 16.7 us  [local(): pl.pallas_call(functools.partial(kernel, n_row, n_col), out_shape=pltpu.V...]
where the time goes in v10:
time: 17.7 us; the launch traced here: 17.5 us
  Pallas kernels  16.7 us (94%)
  local copies, waits for them, and re-layouts  0.8 us (5%)
    pallas_call x1, Pallas kernels, local(): pl.pallas_call(functools.partial(kernel, n_row, n_col), out_shape=pltpu.V...  16.7 us
    unnamed x1, local copies, waits for them, and re-layouts  0.8 us

profile of v10, /device:TPU:0, one launch (start us, length us, event | category | flops | bytes accessed | tf_op | source)
XLA Modules:
  0.0 17.5 jit_solution(16649807039663442708)
XLA Ops:
  0.0 16.7 %shard_map.55 = f32[1024,128]{1,0:T(8,128)S(1)} custom-call(f32[3]{0:T(128)} %mag_hbm.1, f32[3]{0:T(128)} %rate_hbm.1, f32[1024,128]{1,0:T(8,128)} %bitcast.5, s32[1024,128]{1,0:T(8,128)} %bitcast.6, f32[1024,128]{1,0:T(8,128)} %bitcast.7), custom_call_target="tpu_custom_call" | custom-call | flops 20000000 | bytes 2200000 | tf_op jit(solution)/shard_map/pallas_call | solution.py:602
  16.7 0.8 %copy.7 = f32[8,128,128]{2,1,0:T(8,128)} copy(f32[8,128,128]{2,1,0:T(8,128)S(1)} %bitcast.4) | data formatting | bytes 1048576

commit v11 on v9

--- a/solution.py
+++ b/solution.py
@@ -14,7 +14,7 @@
 NZ = 8
 L = 128
 PITCH = L + 8
-BLOCK = 16
+BLOCK = 8
 
 
 def inverse(value):

time: 17.5 us -> 17.5 us (level)
  no operation moved by 1% of the time
where the time goes in v11:
time: 17.5 us; the launch traced here: 17.3 us
  Pallas kernels  16.5 us (94%)
  local copies, waits for them, and re-layouts  0.8 us (5%)
    pallas_call x1, Pallas kernels, local(): pl.pallas_call(functools.partial(kernel, n_row, n_col), out_shape=pltpu.V...  16.5 us
    unnamed x1, local copies, waits for them, and re-layouts  0.8 us

profile of v11, /device:TPU:0, one launch (start us, length us, event | category | flops | bytes accessed | tf_op | source)
XLA Modules:
  0.0 17.3 jit_solution(16179127919242776361)
XLA Ops:
  0.0 16.5 %shard_map.55 = f32[1024,128]{1,0:T(8,128)S(1)} custom-call(f32[3]{0:T(128)} %mag_hbm.1, f32[3]{0:T(128)} %rate_hbm.1, f32[1024,128]{1,0:T(8,128)} %bitcast.5, s32[1024,128]{1,0:T(8,128)} %bitcast.6, f32[1024,128]{1,0:T(8,128)} %bitcast.7), custom_call_target="tpu_custom_call" | custom-call | flops 20000000 | bytes 2200000 | tf_op jit(solution)/shard_map/pallas_call | solution.py:598
  16.5 0.8 %copy.7 = f32[8,128,128]{2,1,0:T(8,128)} copy(f32[8,128,128]{2,1,0:T(8,128)S(1)} %bitcast.4) | data formatting | bytes 1048576
